TPU v7x, 32 devices: a whole 2x2x4 slice. The times are simulated.
32 devices in a mesh: dp: 4 (over z), fsdp: 8 (over y, x, core).
Axes of the slice: x: 2, y: 2, z: 4, core: 2. Of those that a mesh axis runs over, the one named last changes fastest.
Arguments:
- tokens: bfloat16 [98304, 512], P(('dp', 'fsdp')), may hold values from -6 to 6
- lengths: int32 [96], P(('dp', 'fsdp')), may hold values from 256 to 1024, as said below
- w_query: bfloat16 [512, 512], P(None, ('dp', 'fsdp')), may hold values from -0.25 to 0.25
- w_key: bfloat16 [512, 512], P(None, ('dp', 'fsdp')), may hold values from -0.25 to 0.25
- w_value: bfloat16 [512, 512], P(None, ('dp', 'fsdp')), may hold values from -0.25 to 0.25
- w_out: bfloat16 [512, 512], P(None, ('dp', 'fsdp')), may hold values from -6 to 6
- w_up: bfloat16 [512, 2048], P(None, ('dp', 'fsdp')), may hold values from -0.25 to 0.25
- w_down: bfloat16 [2048, 512], P(None, ('dp', 'fsdp')), may hold values from -0.125 to 0.125
- bias_up: bfloat16 [2048], P(('dp', 'fsdp')), may hold values from -3 to 3
- bias_down: bfloat16 [512], P(('dp', 'fsdp')), may hold values from -4 to 4
- gain_attn: bfloat16 [512], P(('dp', 'fsdp')), may hold values from 0.099609375 to 1.8984375
- shift_attn: bfloat16 [512], P(('dp', 'fsdp')), may hold values from -3 to 3
- gain_ffn: bfloat16 [512], P(('dp', 'fsdp')), may hold values from 0.099609375 to 1.8984375
- shift_ffn: bfloat16 [512], P(('dp', 'fsdp')), may hold values from -3 to 3
- cotangent: bfloat16 [98304, 512], P(('dp', 'fsdp')), may hold values from -0.0390625 to 0.0390625
Outputs:
- output: bfloat16 [98304, 512], P(('dp', 'fsdp'))
- grad_tokens: bfloat16 [98304, 512], P(('dp', 'fsdp'))
- grad_w_query: float32 [512, 512], P(None, ('dp', 'fsdp'))
- grad_w_key: float32 [512, 512], P(None, ('dp', 'fsdp'))
- grad_w_value: float32 [512, 512], P(None, ('dp', 'fsdp'))
- grad_w_out: float32 [512, 512], P(None, ('dp', 'fsdp'))
- grad_w_up: float32 [512, 2048], P(None, ('dp', 'fsdp'))
- grad_w_down: float32 [2048, 512], P(None, ('dp', 'fsdp'))
- grad_bias_up: float32 [2048], P(('dp', 'fsdp'))
- grad_bias_down: float32 [512], P(('dp', 'fsdp'))
- grad_gain_attn: float32 [512], P(('dp', 'fsdp'))
- grad_shift_attn: float32 [512], P(('dp', 'fsdp'))
- grad_gain_ffn: float32 [512], P(('dp', 'fsdp'))
- grad_shift_ffn: float32 [512], P(('dp', 'fsdp'))
Inputs may be any that keep to these rules, and one draw needn't show every extreme that they name: `lengths`: each entry is the number of real tokens at the start of a sequence slot of 1024; the rest of the slot is padding. Both ends of the range are taken in every draw.
All inputs are finite; a program needn't handle non-finite values.
Results may differ from a plain program's by a relative error of at most 0.03.
Values may be sent and summed in bfloat16 or wider, within the bound.
No kernel may reach another device: no remote copies, remote signals or barrier semaphores. Data moves between devices by JAX's collectives and lax.ppermute only.
A program may use at most 512 MiB of HBM per device.

v0:
```python
import jax
import jax.numpy as jnp
from jax import lax
from jax.sharding import PartitionSpec as P

D = 512
H = 8
DH = 64
BLOCK = 16
LEVELS = 6
LEN = 1024


def tdot(left, right):
    return lax.dot_general(
        left, right, (((0,), (0,)), ((), ())), preferred_element_type=jnp.float32
    )


def rdot(left, right):
    return lax.dot_general(
        left, right, (((1,), (1,)), ((), ())), preferred_element_type=jnp.float32
    )


def neighbours(values):
    widths = [(0, 0), (1, 1)] + [(0, 0)] * (values.ndim - 2)
    padded = jnp.pad(values, widths)
    return jnp.concatenate([padded[:, :-2], padded[:, 1:-1], padded[:, 2:]], axis=2)


def unneighbour(values):
    width = values.shape[2] // 3
    left_part = values[:, :, :width]
    middle = values[:, :, width : 2 * width]
    right_part = values[:, :, 2 * width :]
    tail = [(0, 0)] * (values.ndim - 2)
    from_left = jnp.pad(left_part[:, 1:], [(0, 0), (0, 1)] + tail)
    from_right = jnp.pad(right_part[:, :-1], [(0, 0), (1, 0)] + tail)
    return middle + from_left + from_right


def pair_mask(level_index, width):
    if level_index == 0:
        return jnp.ones((width, 3 * width), jnp.float32)
    rows_pos = lax.broadcasted_iota(jnp.int32, (width, 3 * width), 0)
    cols_pos = lax.broadcasted_iota(jnp.int32, (width, 3 * width), 1)
    query_half = 2 * rows_pos // width
    key_half = 2 * (cols_pos // width) - 2 + 2 * (cols_pos % width) // width
    return jnp.where(jnp.abs(query_half - key_half) > 1, 1.0, 0.0).astype(jnp.float32)


def halve_mean(values):
    return (values[:, 0::2].astype(jnp.float32) + values[:, 1::2].astype(jnp.float32)) * 0.5


def halve_sum(values):
    return values[:, 0::2].astype(jnp.float32) + values[:, 1::2].astype(jnp.float32)


def normalize(values):
    centred = values - jnp.mean(values, axis=-1, keepdims=True)
    inverse = lax.rsqrt(jnp.mean(centred * centred, axis=-1, keepdims=True) + 1e-05)
    return (centred * inverse, inverse)


def norm_back(gradient, normed, inverse, gain):
    scaled = gradient * gain
    return inverse * (
        scaled
        - jnp.mean(scaled, axis=-1, keepdims=True)
        - normed * jnp.mean(scaled * normed, axis=-1, keepdims=True)
    )


def attend_forward(query, keys, vals, valid):
    seq_count = query.shape[0]
    score_scale = DH ** (-0.5)
    query_now = query
    keys_now = keys
    vals_now = vals * valid[:, :, None, None].astype(jnp.bfloat16)
    valid_now = valid
    stored = []
    numer_list = []
    totals_list = []
    for level_index in range(LEVELS):
        if level_index > 0:
            query_now = halve_mean(query_now)
            keys_now = halve_mean(keys_now)
            vals_now = halve_sum(vals_now)
            valid_now = halve_sum(valid_now)
        length = query_now.shape[1]
        blocks = length // BLOCK
        query_low = query_now.astype(jnp.bfloat16).reshape(seq_count, blocks, BLOCK, H, DH)
        keys_near = neighbours(
            keys_now.astype(jnp.bfloat16).reshape(seq_count, blocks, BLOCK, H, DH)
        )
        vals_near = neighbours(
            vals_now.astype(jnp.bfloat16).reshape(seq_count, blocks, BLOCK, H, DH)
        )
        valid_near = neighbours(valid_now.reshape(seq_count, blocks, BLOCK))
        allowed = pair_mask(level_index, BLOCK)
        weight = allowed[None, None, None] * valid_near[:, :, None, None, :]
        exp_scores = jnp.exp(
            jnp.einsum(
                "snbhd,snchd->snhbc", query_low, keys_near, preferred_element_type=jnp.float32
            )
            * score_scale
        )
        totals = jnp.sum(exp_scores * weight, axis=-1)
        weights_low = (exp_scores * allowed).astype(jnp.bfloat16)
        numerator = jnp.einsum(
            "snhbc,snchd->snbhd", weights_low, vals_near, preferred_element_type=jnp.float32
        )
        stored.append((query_low, keys_near, vals_near, weight, allowed))
        numer_list.append(numerator.reshape(seq_count, length, H, DH))
        totals_list.append(jnp.transpose(totals, (0, 1, 3, 2)).reshape(seq_count, length, H))
    numer_all = numer_list[-1]
    totals_all = totals_list[-1]
    for level_index in range(LEVELS - 2, -1, -1):
        numer_all = jnp.repeat(numer_all, 2, axis=1) + numer_list[level_index]
        totals_all = jnp.repeat(totals_all, 2, axis=1) + totals_list[level_index]
    return (numer_all / totals_all[:, :, :, None], totals_all, stored)


def attend_backward(grad_low, attn, totals_all, stored, valid):
    seq_count = attn.shape[0]
    score_scale = DH ** (-0.5)
    gradient = grad_low.astype(jnp.float32)
    deltas = jnp.sum(gradient * attn, axis=-1)
    numer_grads = [gradient / totals_all[:, :, :, None]]
    totals_grads = [-deltas / totals_all]
    for level_index in range(1, LEVELS):
        numer_grads.append(halve_sum(numer_grads[-1]))
        totals_grads.append(halve_sum(totals_grads[-1]))
    query_grads = []
    keys_grads = []
    vals_grads = []
    for level_index in range(LEVELS):
        query_low, keys_near, vals_near, weight, allowed = stored[level_index]
        blocks = query_low.shape[1]
        length = blocks * BLOCK
        numer_low = (
            numer_grads[level_index].reshape(seq_count, blocks, BLOCK, H, DH).astype(jnp.bfloat16)
        )
        totals_grad = jnp.transpose(
            totals_grads[level_index].reshape(seq_count, blocks, BLOCK, H), (0, 1, 3, 2)
        )
        exp_scores = jnp.exp(
            jnp.einsum(
                "snbhd,snchd->snhbc", query_low, keys_near, preferred_element_type=jnp.float32
            )
            * score_scale
        )
        exp_grads = (
            jnp.einsum(
                "snbhd,snchd->snhbc", numer_low, vals_near, preferred_element_type=jnp.float32
            )
            * allowed
        )
        exp_grads = exp_grads + totals_grad[:, :, :, :, None] * weight
        weights_low = (exp_scores * allowed).astype(jnp.bfloat16)
        vals_near_grad = jnp.einsum(
            "snhbc,snbhd->snchd", weights_low, numer_low, preferred_element_type=jnp.float32
        )
        score_grads = (exp_scores * exp_grads).astype(jnp.bfloat16)
        query_grad = (
            jnp.einsum(
                "snhbc,snchd->snbhd", score_grads, keys_near, preferred_element_type=jnp.float32
            )
            * score_scale
        )
        keys_near_grad = (
            jnp.einsum(
                "snhbc,snbhd->snchd", score_grads, query_low, preferred_element_type=jnp.float32
            )
            * score_scale
        )
        query_grads.append(query_grad.reshape(seq_count, length, H, DH))
        keys_grads.append(unneighbour(keys_near_grad).reshape(seq_count, length, H, DH))
        vals_grads.append(unneighbour(vals_near_grad).reshape(seq_count, length, H, DH))
    query_total = query_grads[-1]
    keys_total = keys_grads[-1]
    vals_total = vals_grads[-1]
    for level_index in range(LEVELS - 2, -1, -1):
        query_total = jnp.repeat(query_total, 2, axis=1) * 0.5 + query_grads[level_index]
        keys_total = jnp.repeat(keys_total, 2, axis=1) * 0.5 + keys_grads[level_index]
        vals_total = jnp.repeat(vals_total, 2, axis=1) + vals_grads[level_index]
    vals_total = vals_total * valid[:, :, None, None]
    return (
        query_total.astype(jnp.bfloat16),
        keys_total.astype(jnp.bfloat16),
        vals_total.astype(jnp.bfloat16),
    )


def on_device(
    tokens,
    lengths,
    w_query,
    w_key,
    w_value,
    w_out,
    w_up,
    w_down,
    bias_up,
    bias_down,
    gain_attn,
    shift_attn,
    gain_ffn,
    shift_ffn,
    cotangent,
):
    whole = (
        lax.all_gather(w_query, ("dp", "fsdp"), axis=1, tiled=True),
        lax.all_gather(w_key, ("dp", "fsdp"), axis=1, tiled=True),
        lax.all_gather(w_value, ("dp", "fsdp"), axis=1, tiled=True),
        lax.all_gather(w_out, ("dp", "fsdp"), axis=1, tiled=True),
        lax.all_gather(w_up, ("dp", "fsdp"), axis=1, tiled=True),
        lax.all_gather(w_down, ("dp", "fsdp"), axis=1, tiled=True),
        lax.all_gather(bias_up, ("dp", "fsdp"), axis=0, tiled=True),
        lax.all_gather(bias_down, ("dp", "fsdp"), axis=0, tiled=True),
        lax.all_gather(gain_attn, ("dp", "fsdp"), axis=0, tiled=True),
        lax.all_gather(shift_attn, ("dp", "fsdp"), axis=0, tiled=True),
        lax.all_gather(gain_ffn, ("dp", "fsdp"), axis=0, tiled=True),
        lax.all_gather(shift_ffn, ("dp", "fsdp"), axis=0, tiled=True),
    )
    (
        full_query,
        full_key,
        full_value,
        full_out,
        full_up,
        full_down,
        full_bias_up,
        full_bias_down,
        full_gain_attn,
        full_shift_attn,
        full_gain_ffn,
        full_shift_ffn,
    ) = whole
    seq_count = lengths.shape[0]
    row_count = tokens.shape[0]
    valid = (lax.broadcasted_iota(jnp.int32, (seq_count, LEN), 1) < lengths[:, None]).astype(
        jnp.float32
    )
    inputs = tokens.astype(jnp.float32)
    normed_one, inverse_one = normalize(inputs)
    normed_attn = (
        normed_one * full_gain_attn.astype(jnp.float32) + full_shift_attn.astype(jnp.float32)
    ).astype(jnp.bfloat16)
    query = jnp.dot(normed_attn, full_query, preferred_element_type=jnp.float32).astype(
        jnp.bfloat16
    )
    keys = jnp.dot(normed_attn, full_key, preferred_element_type=jnp.float32).astype(jnp.bfloat16)
    vals = jnp.dot(normed_attn, full_value, preferred_element_type=jnp.float32).astype(jnp.bfloat16)
    shape_heads = (seq_count, LEN, H, DH)
    attn, totals_all, stored = attend_forward(
        query.reshape(shape_heads), keys.reshape(shape_heads), vals.reshape(shape_heads), valid
    )
    attn_low = attn.reshape(row_count, D).astype(jnp.bfloat16)
    middle = inputs + jnp.dot(attn_low, full_out, preferred_element_type=jnp.float32)
    normed_two, inverse_two = normalize(middle)
    normed_ffn = (
        normed_two * full_gain_ffn.astype(jnp.float32) + full_shift_ffn.astype(jnp.float32)
    ).astype(jnp.bfloat16)
    hidden = jnp.dot(normed_ffn, full_up, preferred_element_type=jnp.float32) + full_bias_up.astype(
        jnp.float32
    )
    sigmoid_hidden = jax.nn.sigmoid(hidden)
    active = (hidden * sigmoid_hidden).astype(jnp.bfloat16)
    output = (
        middle
        + jnp.dot(active, full_down, preferred_element_type=jnp.float32)
        + full_bias_down.astype(jnp.float32)
    ).astype(jnp.bfloat16)
    back_weights = (
        lax.all_gather(w_query, ("dp", "fsdp"), axis=1, tiled=True),
        lax.all_gather(w_key, ("dp", "fsdp"), axis=1, tiled=True),
        lax.all_gather(w_value, ("dp", "fsdp"), axis=1, tiled=True),
        lax.all_gather(w_out, ("dp", "fsdp"), axis=1, tiled=True),
        lax.all_gather(w_up, ("dp", "fsdp"), axis=1, tiled=True),
        lax.all_gather(w_down, ("dp", "fsdp"), axis=1, tiled=True),
        lax.all_gather(bias_up, ("dp", "fsdp"), axis=0, tiled=True),
        lax.all_gather(bias_down, ("dp", "fsdp"), axis=0, tiled=True),
        lax.all_gather(gain_attn, ("dp", "fsdp"), axis=0, tiled=True),
        lax.all_gather(shift_attn, ("dp", "fsdp"), axis=0, tiled=True),
        lax.all_gather(gain_ffn, ("dp", "fsdp"), axis=0, tiled=True),
        lax.all_gather(shift_ffn, ("dp", "fsdp"), axis=0, tiled=True),
    )
    (
        back_query,
        back_key,
        back_value,
        back_out,
        back_up,
        back_down,
        back_bias_up,
        back_bias_down,
        back_gain_attn,
        back_shift_attn,
        back_gain_ffn,
        back_shift_ffn,
    ) = back_weights
    grad_down = tdot(active, cotangent)
    grad_bias_down = jnp.sum(cotangent.astype(jnp.float32), axis=0)
    grad_active = rdot(cotangent, back_down)
    slope = sigmoid_hidden * (1.0 + hidden * (1.0 - sigmoid_hidden))
    grad_hidden = (grad_active * slope).astype(jnp.bfloat16)
    grad_up = tdot(normed_ffn, grad_hidden)
    grad_bias_up = jnp.sum(grad_hidden.astype(jnp.float32), axis=0)
    grad_nffn = rdot(grad_hidden, back_up)
    grad_gain_ffn = jnp.sum(grad_nffn * normed_two, axis=0)
    grad_shift_ffn = jnp.sum(grad_nffn, axis=0)
    grad_middle = cotangent.astype(jnp.float32) + norm_back(
        grad_nffn, normed_two, inverse_two, back_gain_ffn.astype(jnp.float32)
    )
    grad_middle_low = grad_middle.astype(jnp.bfloat16)
    grad_out = tdot(attn_low, grad_middle_low)
    grad_attn = rdot(grad_middle_low, back_out).astype(jnp.bfloat16)
    grad_query4, grad_keys4, grad_vals4 = attend_backward(
        grad_attn.reshape(shape_heads), attn, totals_all, stored, valid
    )
    grad_query_rows = grad_query4.reshape(row_count, D)
    grad_keys_rows = grad_keys4.reshape(row_count, D)
    grad_vals_rows = grad_vals4.reshape(row_count, D)
    grad_query = tdot(normed_attn, grad_query_rows)
    grad_key = tdot(normed_attn, grad_keys_rows)
    grad_value = tdot(normed_attn, grad_vals_rows)
    grad_nattn = (
        rdot(grad_query_rows, back_query)
        + rdot(grad_keys_rows, back_key)
        + rdot(grad_vals_rows, back_value)
    )
    grad_gain_attn = jnp.sum(grad_nattn * normed_one, axis=0)
    grad_shift_attn = jnp.sum(grad_nattn, axis=0)
    grad_tokens = (
        grad_middle
        + norm_back(grad_nattn, normed_one, inverse_one, back_gain_attn.astype(jnp.float32))
    ).astype(jnp.bfloat16)
    all_shares = (
        lax.psum_scatter(grad_query, ("dp", "fsdp"), scatter_dimension=1, tiled=True),
        lax.psum_scatter(grad_key, ("dp", "fsdp"), scatter_dimension=1, tiled=True),
        lax.psum_scatter(grad_value, ("dp", "fsdp"), scatter_dimension=1, tiled=True),
        lax.psum_scatter(grad_out, ("dp", "fsdp"), scatter_dimension=1, tiled=True),
        lax.psum_scatter(grad_up, ("dp", "fsdp"), scatter_dimension=1, tiled=True),
        lax.psum_scatter(grad_down, ("dp", "fsdp"), scatter_dimension=1, tiled=True),
        lax.psum_scatter(grad_bias_up, ("dp", "fsdp"), scatter_dimension=0, tiled=True),
        lax.psum_scatter(grad_bias_down, ("dp", "fsdp"), scatter_dimension=0, tiled=True),
        lax.psum_scatter(grad_gain_attn, ("dp", "fsdp"), scatter_dimension=0, tiled=True),
        lax.psum_scatter(grad_shift_attn, ("dp", "fsdp"), scatter_dimension=0, tiled=True),
        lax.psum_scatter(grad_gain_ffn, ("dp", "fsdp"), scatter_dimension=0, tiled=True),
        lax.psum_scatter(grad_shift_ffn, ("dp", "fsdp"), scatter_dimension=0, tiled=True),
    )
    return (
        output,
        grad_tokens,
        all_shares[0],
        all_shares[1],
        all_shares[2],
        all_shares[3],
        all_shares[4],
        all_shares[5],
        all_shares[6],
        all_shares[7],
        all_shares[8],
        all_shares[9],
        all_shares[10],
        all_shares[11],
    )


def solution(mesh):
    placed = (
        P(("dp", "fsdp"), None),
        P(("dp", "fsdp")),
        P(None, ("dp", "fsdp")),
        P(None, ("dp", "fsdp")),
        P(None, ("dp", "fsdp")),
        P(None, ("dp", "fsdp")),
        P(None, ("dp", "fsdp")),
        P(None, ("dp", "fsdp")),
        P(("dp", "fsdp")),
        P(("dp", "fsdp")),
        P(("dp", "fsdp")),
        P(("dp", "fsdp")),
        P(("dp", "fsdp")),
        P(("dp", "fsdp")),
        P(("dp", "fsdp"), None),
    )
    return jax.shard_map(
        on_device,
        mesh=mesh,
        in_specs=placed,
        out_specs=(
            P(("dp", "fsdp"), None),
            P(("dp", "fsdp"), None),
            P(None, ("dp", "fsdp")),
            P(None, ("dp", "fsdp")),
            P(None, ("dp", "fsdp")),
            P(None, ("dp", "fsdp")),
            P(None, ("dp", "fsdp")),
            P(None, ("dp", "fsdp")),
            P(("dp", "fsdp")),
            P(("dp", "fsdp")),
            P(("dp", "fsdp")),
            P(("dp", "fsdp")),
            P(("dp", "fsdp")),
            P(("dp", "fsdp")),
        ),
        check_vma=False,
    )
```

profile of v0, /device:TPU:0, one launch (start us, length us, event | category | flops | bytes accessed | tf_op | source)
XLA Modules:
  0.0 1896.5 jit_solution(4995525221549350492)
XLA Ops:
  17.8 42.3 %all-reduce.55 = (bf16[512]{0:T(512)(128)(2,1)S(1)}, bf16[512]{0:T(512)(128)(2,1)S(1)}, bf16[512]{0:T(512)(128)(2,1)S(1)}, bf16[512]{0:T(512)(128)(2,1)S(1)}, bf...) all-reduce(bf16[512]{0:T(512)(128)(2,1)S(1)} %dynamic-update-slice., ...), channel_id=1, replica_groups=mesh['dp'=4,'fsdp'=8] {'dp','fsdp'}, use_global_device_ids=true, to_apply=%add.43 | all-reduce | flops 4608 | bytes 18432
  60.1 45.4 %all_gather.47 = bf16[512,512]{0,1:T(8,128)(2,1)} all-gather(bf16[512,16]{0,1:T(8,128)(2,1)} %param.17), channel_id=1, replica_groups=mesh['dp'=4,'fsdp'=8] {'dp','fsdp'}, dimensions={1}, use_global_device_ids=true | all-gather | bytes 540672 | tf_op jit(solution)/shard_map/all_gather | solution.py:215
  117.5 9.0 reshape_reshape.6
  132.1 38.2 %all_gather.46 = bf16[512,512]{0,1:T(8,128)(2,1)S(1)} all-gather(bf16[512,16]{0,1:T(8,128)(2,1)S(1)} %copy-done.148), channel_id=1, replica_groups=mesh['dp'=4,'fsdp'=8] {'dp','fsdp'}, dimensions={1}, use_global_device_ids=true | all-gather | bytes 540672 | tf_op jit(solution)/shard_map/all_gather | solution.py:217
  186.1 39.4 %all_gather.48 = bf16[512,512]{0,1:T(8,128)(2,1)S(1)} all-gather(bf16[512,16]{0,1:T(8,128)(2,1)S(1)} %copy-done.149), channel_id=1, replica_groups=mesh['dp'=4,'fsdp'=8] {'dp','fsdp'}, dimensions={1}, use_global_device_ids=true | all-gather | bytes 540672 | tf_op jit(solution)/shard_map/all_gather | solution.py:216
  248.5 40.9 %all_gather.49 = bf16[512,512]{0,1:T(8,128)(2,1)} all-gather(bf16[512,16]{0,1:T(8,128)(2,1)} %param.20), channel_id=1, replica_groups=mesh['dp'=4,'fsdp'=8] {'dp','fsdp'}, dimensions={1}, use_global_device_ids=true | all-gather | bytes 540672 | tf_op jit(solution)/shard_map/all_gather | solution.py:218
  379.1 9.1 multiply_reduce_fusion.5
  391.5 6.9 fusion.39
  411.5 11.6 reshape.582
  423.1 12.9 pad_slice_fusion.1
  437.1 7.3 pad_slice_fusion.3
  444.6 18.5 multiply_reduce_fusion.1
  465.1 7.0 div.319
  472.1 11.5 reshape.646
  483.6 17.4 fusion.28
  501.1 15.4 copy.828
  516.5 11.6 reshape.584
  528.2 9.1 divide_convert_fusion
  544.1 21.2 %multiply_convert_fusion.1 = (bf16[3072,2048]{1,0:T(8,128)(2,1)}, f32[3072,2048]{1,0:T(8,128)}) fusion(f32[2048]{0:T(1024)S(1)} %copy-done.151, bf16[512,2048]{0,1:T(8,128)(2,1)} %all-gather.3.cloned.1.call-done, f32[3072,512]{0,1:T(8,128)} %copy-done.3, f32[512]{0:T(512)S(1)} %copy-done.155, f32[512]{0:T(512)S(1)} %copy-done.146, ...), kind=kOutput, calls=%fused_computation.3 | convolution fusion | flops 6488064000 | bytes 46174208 | tf_op jit(solution)/shard_map/dot_general | solution.py:267
  565.4 19.7 %convert_reduce_fusion = (f32[2048]{0:T(1024)}, bf16[3072,2048]{1,0:T(8,128)(2,1)}) fusion(f32[3072,2048]{1,0:T(8,128)} %get-tuple-element.250, f32[2048]{0:T(1024)S(1)} %copy-done.151, bf16[3072,512]{1,0:T(8,128)(2,1)S(1)} %copy-done.46, bf16[2048,512]{0,1:T(8,128)(2,1)} %all-gather.5.cloned.1.call-done), kind=kOutput, calls=%fused_computation.1 | convolution fusion | flops 6517946368 | bytes 43008000 | tf_op jit(solution)/shard_map/dot_general | solution.py:21
  585.1 12.0 fusion.159
  603.9 7.2 multiply_reduce_fusion.2
  622.2 7.3 fusion.27
  629.5 10.2 reshape.631
  639.8 10.4 reshape.649
  650.1 48.0 %broadcast_divide_fusion = (f32[3,1024,8,64]{3,2,1,0:T(8,128)}, f32[3,1024,8]{2,1,0:T(8,128)S(1)}) fusion(f32[3,1024,8,64]{3,2,1,0:T(8,128)} %reshape.649, f32[3,1024,8]{2,1,0:T(8,128)S(1)} %copy-done.14, f32[3,1024,8,64]{3,2,1,0:T(8,128)} %bitcast.215, f32[3,1024,8,64]{3,2,1,0:T(8,128)} %bitcast.216), kind=kLoop, calls=%fused_computation.67 | loop fusion | flops 7839744 | bytes 25362432 | tf_op jit(solution)/shard_map/div | solution.py:131
  709.2 8.1 fusion.132
  760.6 8.0 convolution_bitcast_fusion.1
  768.6 10.4 multiply_convert_fusion.4
  779.0 10.8 multiply_bitcast_fusion.4
  789.8 8.1 multiply_bitcast_fusion.1
  798.0 8.5 copy.874
  814.9 24.3 %convolution_bitcast_fusion = f32[3,64,48,8,64]{4,2,3,1,0:T(8,128)} fusion(f32[3,64,8,16,48]{4,3,2,1,0:T(8,128)} %get-tuple-element.246, f32[3,64,16,8,64]{4,3,2,1,0:T(8,128)} %reshape.631, f32[3,64,16,8]{2,3,1,0:T(8,128)S(1)} %copy.879), kind=kOutput, calls=%fused_computation.8 | convolution fusion | flops 156499968 | bytes 29982720 | tf_op jit(solution)/shard_map/snhbc,snbhd->snchd/dot_general | solution.py:163
  839.2 20.2 %multiply_convert_fusion.2 = bf16[3,64,8,16,48]{4,3,2,1,0:T(8,128)(2,1)} fusion(f32[3,64,8,16,48]{4,3,2,1,0:T(8,128)} %get-tuple-element.246, f32[3,64,8,16]{3,2,1,0:T(8,128)} %copy.882, f32[3,64,48]{2,1,0:T(8,128)S(1)} %copy-done.139, bf16[3,64,16,8,64]{4,2,3,1,0:T(8,128)(2,1)} %get-tuple-element.174, bf16[3,64,16,8,64]{4,2,3,1,0:T(8,128)(2,1)} %copy-done.6, ...), kind=kOutput, calls=%fused_computation.16 | convolution fusion | flops 188350464 | bytes 23040000 | tf_op jit(solution)/shard_map/snbhd,snchd->snhbc/dot_general | solution.py:156
  859.5 11.9 multiply_bitcast_fusion.2
  871.3 15.4 copy.883
  886.8 11.5 reshape.613
  995.1 8.1 broadcast_in_dim.160
  1003.2 11.5 mul.913
  1025.2 11.0 fusion.147
  1036.3 9.0 fusion.148
  1045.3 14.8 fusion.145
  1068.0 10.1 fusion.23
  1084.0 15.2 fusion
  1129.2 11.5 reshape.628
  1140.6 8.5 copy.899
  1165.7 15.3 copy.917
  1181.1 11.5 reshape.629
  1192.6 17.7 multiply_bitcast_fusion
  1225.5 11.5 mul.945
  1241.8 18.5 fusion.146
  1260.3 19.2 %fusion.1 = f32[3,64,16,8,64]{4,2,3,1,0:T(8,128)} fusion(f32[3,64,48,8,64]{4,2,3,1,0:T(8,128)} %multiply_bitcast_fusion, f32[3,63,16,8,64]{4,2,3,1,0:T(8,128)} %get-tuple-element.162, f32[3,63,16,8,64]{4,2,3,1,0:T(8,128)} %get-tuple-element.161), kind=kLoop, calls=%fused_computation.12 | loop fusion | flops 3145728 | bytes 24969216 | tf_op jit(solution)/shard_map/add | solution.py:40
  1279.5 15.4 copy.904
  1294.9 11.5 reshape.618
  1317.0 11.0 fusion.165
  1328.2 13.3 fusion.128
  1341.6 13.9 add_convert_fusion.2
  1366.3 7.3 fusion.21
  1373.6 37.3 %all-reduce.54 = (f32[2048]{0:T(1024)S(1)}, f32[512]{0:T(512)S(1)}, f32[512]{0:T(512)S(1)}, f32[512]{0:T(512)S(1)}, f32[512]{0:T(512)S(1)}, /*index=5*/f32[512]{0:T(512)S(1)}) all-reduce(f32[2048]{0:T(1024)S(1)} %copy-done.152, f32[512]{0:T(512)S(1)} %copy-done.153, ...), channel_id=8, replica_groups=mesh['dp'=4,'fsdp'=8] {'dp','fsdp'}, use_global_device_ids=true, to_apply=%region_22.23.clone | all-reduce | flops 4608 | bytes 36864
  1413.8 7.2 fusion.20
  1426.3 50.0 %reduce-scatter.11.cloned.1.call-done = f32[512,16]{0,1:T(8,128)} async-done(((f32[512,512]{0,1:T(8,128)}), f32[512,16]{0,1:T(8,128)}) %reduce-scatter.11.cloned.1.call-update) | async-done | bytes 32784 | tf_op jit(solution)/shard_map/reduce_scatter | solution.py:344
  1476.3 133.6 %reduce-scatter.9.cloned.1.call-done = f32[512,16]{0,1:T(8,128)} async-done(((f32[512,512]{0,1:T(8,128)}), f32[512,16]{0,1:T(8,128)}) %reduce-scatter.9.cloned.1.call-update) | async-done | bytes 32784 | tf_op jit(solution)/shard_map/reduce_scatter | solution.py:343
  1609.9 139.8 %reduce-scatter.17.cloned.1.call-done = f32[2048,16]{0,1:T(8,128)} async-done(((f32[2048,512]{0,1:T(8,128)}), f32[2048,16]{0,1:T(8,128)}) %reduce-scatter.17.cloned.1.call-update) | async-done | bytes 131088 | tf_op jit(solution)/shard_map/reduce_scatter | solution.py:347
  1749.8 139.7 %reduce-scatter.15.cloned.1.call-done = f32[512,64]{0,1:T(8,128)} async-done(((f32[512,2048]{0,1:T(8,128)}), f32[512,64]{0,1:T(8,128)}) %reduce-scatter.15.cloned.1.call-update) | async-done | bytes 131088 | tf_op jit(solution)/shard_map/reduce_scatter | solution.py:346
  (712 shorter events, 478.5 us)
Async XLA Ops:
  7.2 536.9 %all-gather.3.cloned.1.call-start = ((), (), s32[]{:S(2)}) async-start(), calls=%async_computation.6 | async-start | bytes 2162688 | tf_op jit(solution)/shard_map/all_gather | solution.py:219
  7.9 557.4 %all-gather.5.cloned.1.call-start = ((), (), s32[]{:S(2)}) async-start(), calls=%async_computation.7 | async-start | bytes 2162688 | tf_op jit(solution)/shard_map/all_gather | solution.py:220
  8.7 1417.6 %reduce-scatter.13.cloned.1.call-start = ((), (), s32[]{:S(2)}) async-start(), calls=%async_computation.11 | async-start | bytes 1081344 | tf_op jit(solution)/shard_map/reduce_scatter | solution.py:345
  60.1 50.1 %copy-start.144 = (f32[512]{0:T(512)}, f32[512]{0:T(512)S(1)}, u32[]{:S(2)}) copy-start(f32[512]{0:T(512)S(1)} %convert_element_type.325) | copy-start | bytes 6148
  117.5 9.0 copy-start.26
  241.4 49.2 %copy-start.45 = (bf16[3072,512]{1,0:T(8,128)(2,1)S(1)}, bf16[3072,512]{1,0:T(8,128)(2,1)}, u32[]{:S(2)}) copy-start(bf16[3072,512]{1,0:T(8,128)(2,1)} %param.29) | copy-start | bytes 9437188
  243.5 148.0 %copy-start.79 = (f32[16,48]{1,0:T(8,128)}, f32[16,48]{1,0:T(8,128)S(1)}, u32[]{:S(2)}) copy-start(f32[16,48]{1,0:T(8,128)S(1)} %fusion.92) | copy-start | bytes 9220
  246.2 53.0 %copy-start.83 = (f32[3,64,16]{2,1,0:T(8,128)}, f32[3,64,16]{2,1,0:T(8,128)S(1)}, u32[]{:S(2)}) copy-start(f32[3,64,16]{2,1,0:T(8,128)S(1)} %get-tuple-element.224) | copy-start | bytes 36868
  310.8 64.2 %copy-start.15 = (bf16[3,32,16,8,64]{4,2,3,1,0:T(8,128)(2,1)}, bf16[3,32,16,8,64]{4,2,3,1,0:T(8,128)(2,1)S(1)}, u32[]{:S(2)}) copy-start(bf16[3,32,16,8,64]{4,2,3,1,0:T(8,128)(2,1)S(1)} %copy.818) | copy-start | bytes 4718596
  312.3 32.3 %copy-start.66 = (bf16[3,4,16,8,64]{4,2,3,1,0:T(8,128)(2,1)}, bf16[3,4,16,8,64]{4,2,3,1,0:T(8,128)(2,1)S(1)}, u32[]{:S(2)}) copy-start(bf16[3,4,16,8,64]{4,2,3,1,0:T(8,128)(2,1)S(1)} %copy.800) | copy-start | bytes 589828
  315.8 7.6 slice-start.11
  379.0 9.4 copy-start.123
  379.0 9.5 copy-start.109
  379.0 9.6 copy-start.93
  411.5 24.5 %slice-start.5 = ((s8[6291456]{0:T(1024)(128)(4,1)}), s8[2097152]{0:T(1024)(128)(4,1)S(1)}, s32[]{:S(2)}) async-start(s8[6291456]{0:T(1024)(128)(4,1)} %bitcast.221), calls=%async_computation.19 | async-start | bytes 4194304
  423.1 12.9 slice-start.6
  423.1 12.9 copy-start.120
  437.1 7.4 copy-start.6
  444.6 18.5 copy-start.138
  464.6 7.5 copy-start.81
  528.1 9.1 copy-start.1
  540.6 70.5 %copy-start.133 = (f32[3072]{0:T(1024)}, f32[3072]{0:T(1024)S(1)}, u32[]{:S(2)}) copy-start(f32[3072]{0:T(1024)S(1)} %broadcast_multiply_fusion.16) | copy-start | bytes 36868
  544.0 67.1 %copy-start.135 = (f32[3072]{0:T(1024)}, f32[3072]{0:T(1024)S(1)}, u32[]{:S(2)}) copy-start(f32[3072]{0:T(1024)S(1)} %add_rsqrt_fusion) | copy-start | bytes 36868
  544.0 21.3 %copy-start.46 = (bf16[3072,512]{1,0:T(8,128)(2,1)S(1)}, bf16[3072,512]{1,0:T(8,128)(2,1)}, u32[]{:S(2)}) copy-start(bf16[3072,512]{1,0:T(8,128)(2,1)} %param.29) | copy-start | bytes 9437188
  565.4 19.7 %copy-start.159 = (bf16[512,2048]{0,1:T(8,128)(2,1)S(1)}, bf16[512,2048]{0,1:T(8,128)(2,1)}, u32[]{:S(2)}) copy-start(bf16[512,2048]{0,1:T(8,128)(2,1)} %all-gather.3.cloned.1.call-done) | copy-start | bytes 6291460
  597.1 14.0 slice-start
  603.9 7.7 copy-start.5
  611.6 7.9 copy-start.12
  639.8 10.4 copy-start.14
  650.1 48.4 %copy-start.82 = (f32[3,1024,8]{1,2,0:T(8,128)S(1)}, f32[3,1024,8]{1,2,0:T(8,128)}, u32[]{:S(2)}) copy-start(f32[3,1024,8]{1,2,0:T(8,128)} %copy-done.81) | copy-start | bytes 294916
  709.2 8.1 copy-start.141
  753.0 7.6 slice-start.19
  760.6 8.0 copy-start.87
  779.0 10.8 copy-start.21
  779.0 10.8 copy-start.44
  798.0 628.3 %reduce-scatter.7.cloned.1.call-start = ((), (), s32[]{:S(2)}) async-start(), calls=%async_computation.8 | async-start | bytes 1081344 | tf_op jit(solution)/shard_map/reduce_scatter | solution.py:342
  814.9 24.3 %copy-start.139 = (f32[3,64,48]{2,1,0:T(8,128)S(1)}, f32[3,64,48]{2,1,0:T(8,128)}, u32[]{:S(2)}) copy-start(f32[3,64,48]{2,1,0:T(8,128)} %copy-done.138) | copy-start | bytes 110596
  814.9 44.6 %slice-start.9 = ((s8[6291456]{0:T(1024)(128)(4,1)}), s8[2097152]{0:T(1024)(128)(4,1)S(1)}, s32[]{:S(2)}) async-start(s8[6291456]{0:T(1024)(128)(4,1)} %bitcast.229), calls=%async_computation.23 | async-start | bytes 4194304
  839.2 20.2 %slice-start.10 = ((s8[6291456]{0:T(1024)(128)(4,1)}), s8[4194304]{0:T(1024)(128)(4,1)S(1)}, s32[]{:S(2)}) async-start(s8[6291456]{0:T(1024)(128)(4,1)} %bitcast.229), calls=%async_computation.24 | async-start | bytes 8388608
  911.9 10.6 copy-start.30
  931.6 9.8 slice-start.17
  933.8 7.5 slice-start.18
  969.9 12.8 slice-start.2
  969.9 12.8 slice-start.3
  1014.7 7.7 copy-start.55
  1045.3 14.8 copy-start.39
  1045.3 14.8 copy-start.40
  1062.3 15.8 slice-start.15
  1068.0 10.1 slice-start.16
  1084.0 15.2 copy-start.60
  1084.0 15.2 copy-start.61
  1192.6 17.8 copy-start.140
  1210.3 266.0 %reduce-scatter.11.cloned.1.call-start = ((), (), s32[]{:S(2)}) async-start(), calls=%async_computation.10 | async-start | bytes 1081344 | tf_op jit(solution)/shard_map/reduce_scatter | solution.py:344
  1215.8 21.2 %copy-start.23 = (bf16[3072,512]{1,0:T(8,128)(2,1)}, bf16[3072,512]{1,0:T(8,128)(2,1)S(1)}, u32[]{:S(2)}) copy-start(bf16[3072,512]{1,0:T(8,128)(2,1)S(1)} %multiply_convert_fusion.3) | copy-start | bytes 9437188
  1260.3 349.6 %reduce-scatter.9.cloned.1.call-start = ((), (), s32[]{:S(2)}) async-start(), calls=%async_computation.9 | async-start | bytes 1081344 | tf_op jit(solution)/shard_map/reduce_scatter | solution.py:343
  1306.4 7.5 copy-start.56
  1316.8 433.0 %reduce-scatter.17.cloned.1.call-start = ((), (), s32[]{:S(2)}) async-start(), calls=%async_computation.13 | async-start | bytes 4325376 | tf_op jit(solution)/shard_map/reduce_scatter | solution.py:347
  1317.0 11.2 copy-start.134
  1317.0 11.2 copy-start.136
  1317.0 11.2 copy-start.147
  1317.0 11.2 copy-start.156
  1328.1 13.4 copy-start.157
  1328.1 13.5 copy-start.158
  1328.1 561.3 %reduce-scatter.15.cloned.1.call-start = ((), (), s32[]{:S(2)}) async-start(), calls=%async_computation.12 | async-start | bytes 4325376 | tf_op jit(solution)/shard_map/reduce_scatter | solution.py:346
  (125 other events, 486.3 us)
Sparse Core Ops, SparseCore 0:
  10.9 59.2 all-gather.2
  73.0 55.2 all-gather.4
  798.1 132.2 reduce-scatter.12
  1210.4 132.3 reduce-scatter.6
  1345.5 130.7 reduce-scatter.10
  1479.0 130.8 reduce-scatter.8
  1612.8 136.9 reduce-scatter.16
  1752.6 136.7 reduce-scatter.14
where the time goes:
time: 1910 us; the launch traced here: 1900 us
  local copies, waits for them, and re-layouts  570 us (30%)
  waiting for transfers between devices  465 us (24%)
  matrix products  360 us (19%)
  blocking collectives  244 us (13%)
  other arithmetic  240 us (13%)
    reduce_scatter x1, waiting for transfers between devices, on_device(): lax.psum_scatter(grad_down, ('dp', 'fsdp'), scatter_dimension=1, tiled=True)  140 us
    reduce_scatter x1, waiting for transfers between devices, on_device(): lax.psum_scatter(grad_up, ('dp', 'fsdp'), scatter_dimension=1, tiled=True)  140 us
    reduce_scatter x1, waiting for transfers between devices, on_device(): lax.psum_scatter(grad_key, ('dp', 'fsdp'), scatter_dimension=1, tiled=True)  134 us
    unnamed x2, blocking collectives  79.5 us
    slice x12, local copies, waits for them, and re-layouts, unneighbour(): from_left = jnp.pad(left_part[:, 1:], [(0, 0), (0, 1)] + tail)  65.3 us
    add x11, other arithmetic, unneighbour(): return middle + from_left + from_right  61.2 us
    add x11, local copies, waits for them, and re-layouts, unneighbour(): return middle + from_left + from_right  52.6 us
    dot_general x6, matrix products, rdot(): lax.dot_general(left, right, (((1,), (1,)), ((), ())), preferred_element_...  51.3 us
  transfers between devices with their start and end apart: 8, of which 4 were waited for; matrix products, arithmetic and copies ran while one was open for 49% of the time, Pallas kernels for 0%

commit v1 on v0

v1 whole, which is shorter than its diff:
```python
import functools

import jax
import jax.numpy as jnp
import numpy as np
from jax import lax
from jax.experimental import pallas as pl
from jax.experimental.pallas import tpu as pltpu
from jax.sharding import PartitionSpec as P

D = 512
H = 8
DH = 64
FF = 2048
BLOCK = 16
LEVELS = 6
LEN = 1024
AXES = ("dp", "fsdp")
BF16 = jnp.bfloat16
F32 = jnp.float32

STARTS = (32, 1072, 1600, 1872, 2016, 2096)
SIZES = tuple(LEN >> level for level in range(LEVELS))
ROWS = 2192
GAPS = ((0, 32), (1056, 16), (1584, 16), (1856, 16), (2000, 16), (2080, 16), (2128, 64))
WINDOWS = 32
QUERIES = 64
KEYS = 128
UNROLL = 8
POOL_CHUNK = 256
SHARE = 16
FIRST_ROWS = 3 * SHARE + 8
SECOND_ROWS = 9 * SHARE + 8
SCORE = 0.125 * 1.4426950408889634


def nn(left, right):
    return lax.dot_general(left, right, (((1,), (0,)), ((), ())), preferred_element_type=F32)


def nt(left, right):
    return lax.dot_general(left, right, (((1,), (1,)), ((), ())), preferred_element_type=F32)


def tn(left, right):
    return lax.dot_general(left, right, (((0,), (0,)), ((), ())), preferred_element_type=F32)


def score_bias():
    query = (np.arange(2 * QUERIES) % QUERIES)[:, None]
    key = np.arange(KEYS)[None, :] - 32
    near = np.abs(query // 16 - key // 16) <= 1
    apart = np.abs(query // 8 - key // 8) > 1
    return np.where(np.stack([near, near & apart]), 0.0, -1e30).astype(np.float32)


def pool_matrix():
    matrix = np.zeros((POOL_CHUNK, POOL_CHUNK), np.float32)
    first = 0
    for level in range(1, LEVELS):
        count = POOL_CHUNK >> level
        for row in range(count):
            matrix[first + row, row << level : (row + 1) << level] = 0.5**level
        first += count
    return matrix


def halves():
    lane = np.arange(128)
    return np.stack([lane < DH, lane >= DH]).astype(np.float32)


def window_row(window):
    gaps = sum((window >= first).astype(jnp.int32) for first in (16, 24, 28, 30, 31))
    return pl.multiple_of(STARTS[0] + QUERIES * window + 16 * gaps, 16)


def window_loop(step, unroll=UNROLL):
    def body(index, carry):
        for inner in range(unroll):
            window = index * unroll + inner
            row = window_row(window)
            step(
                pl.ds(row, QUERIES),
                pl.ds(pl.multiple_of(row - 32, 16), KEYS),
                pl.ds(pl.multiple_of(window * 2 * QUERIES, 128), 2 * QUERIES),
                jnp.where(window >= 16, 1, 0),
            )
        return carry

    lax.fori_loop(0, WINDOWS // unroll, body, 0)


def row_loop(total, size, step, unroll=1):
    def body(index, carry):
        for inner in range(unroll):
            step(pl.multiple_of((index * unroll + inner) * size, size))
        return carry

    lax.fori_loop(0, total // (size * unroll), body, 0)


def pair_lanes(pair):
    return slice(128 * pair, 128 * pair + 128)


def by_head(values, half):
    return jnp.concatenate([values * half[0:1, :], values * half[1:2, :]], axis=0)


def joined_heads(values, low_head):
    return jnp.where(low_head, values[:QUERIES], values[QUERIES:])


def fill_counts(counts, length):
    clear_gaps(counts)
    for level in range(LEVELS):
        place = lax.broadcasted_iota(jnp.int32, (SIZES[level], 128), 0)
        span = 1 << level
        number = jnp.clip(length - place * span, 0, span).astype(F32)
        counts[STARTS[level] : STARTS[level] + SIZES[level], :] = number.astype(BF16)


def block_places(place, plain, sign):
    for half in range(2):
        for block in range(16):
            if plain:
                yield half, block, half * 16 + block
            else:
                column = place[1] ^ (half + 2 * (block // 4))
                row = (place[0] + 4 + sign * (block % 4)) % 4
                yield half, block, row * 8 + column


def sixteen(device):
    return pl.ds(pl.multiple_of(device * SHARE, SHARE), SHARE)


def sixty_four(device):
    return pl.ds(pl.multiple_of(device * 4 * SHARE, 4 * SHARE), 4 * SHARE)


def load_first(place, plain, blocks, weights, vectors):
    total = jnp.zeros((8, D), F32)
    for half, block, device in block_places(place, plain, -1):
        source = blocks[half]
        for part in range(3):
            rows = pl.ds(pl.multiple_of(part * D + device * SHARE, SHARE), SHARE)
            weights[rows, :] = source[block, part * SHARE : part * SHARE + SHARE, :]
        total = total + source[block, 3 * SHARE : 3 * SHARE + 8, :].astype(F32)
    vectors[...] = total


def load_second(place, plain, blocks, w_out, w_up, w_down, vectors):
    total = jnp.zeros((8, D), F32)
    for half, block, device in block_places(place, plain, -1):
        source = blocks[half]
        w_out[sixteen(device), :] = source[block, 0:SHARE, :]
        w_up[sixty_four(device), :] = source[block, SHARE : 5 * SHARE, :]
        for part in range(4):
            at = (5 + part) * SHARE
            w_down[sixteen(device), D * part : D * part + D] = source[block, at : at + SHARE, :]
        total = total + source[block, 9 * SHARE : 9 * SHARE + 8, :].astype(F32)
    vectors[...] = total


def layer_norm(values):
    mean = jnp.mean(values, axis=-1, keepdims=True)
    centred = values - mean
    inverse = lax.rsqrt(jnp.mean(centred * centred, axis=-1, keepdims=True) + 1e-05)
    return centred * inverse, inverse


def norm_back(gradient, normed, inverse, gain):
    scaled = gradient * gain
    return inverse * (
        scaled
        - jnp.mean(scaled, axis=-1, keepdims=True)
        - normed * jnp.mean(scaled * normed, axis=-1, keepdims=True)
    )


def clear_gaps(ref):
    for first, count in GAPS:
        ref[first : first + count, :] = jnp.zeros((count, ref.shape[1]), ref.dtype)


def spread_up(ref, factor):
    for level in range(LEVELS - 2, -1, -1):
        count = SIZES[level + 1]
        size = min(count, 64)

        def step(first, level=level, size=size):
            for pair in range(4):
                above = ref[pair, pl.ds(STARTS[level + 1] + first, size), :]
                if factor != 1.0:
                    above = above * factor
                for odd in (0, 1):
                    below = pl.ds(STARTS[level] + 2 * first + odd, size, stride=2)
                    ref[pair, below, :] = ref[pair, below, :] + above

        row_loop(count, size, step)


def attend_kernel(
    plain,
    lengths,
    place,
    tokens,
    near_blocks,
    far_blocks,
    bias,
    pool,
    half,
    query,
    key,
    value,
    probs,
    attn,
    total,
    weights,
    vectors,
    normed,
    joined,
    top,
    counts,
    numer,
    denom,
):
    @pl.when(pl.program_id(0) == 0)
    def _():
        load_first(place, plain, (near_blocks, far_blocks), weights, vectors)

    length = lengths[pl.program_id(0)]
    gain = vectors[0:1, :]
    shift = vectors[1:2, :]

    def norm_step(first):
        rows = pl.ds(first, 64)
        values, _ = layer_norm(tokens[rows, :].astype(F32))
        normed[rows, :] = (values * gain + shift).astype(BF16)

    row_loop(LEN, 64, norm_step, 4)
    for ref in (query, key, value):
        clear_gaps(ref)
    fill_counts(counts, length)
    targets = ((query, 0), (key, D), (value, 2 * D))
    for first in range(0, LEN, POOL_CHUNK):
        rows = slice(first, first + POOL_CHUNK)
        chunk = first // POOL_CHUNK
        values = nt(normed[rows, :], weights[...])
        valid = (lax.broadcasted_iota(jnp.int32, (POOL_CHUNK, 1), 0) + first < length).astype(F32)
        joined[rows, : 2 * D] = values[:, : 2 * D].astype(BF16)
        joined[rows, 2 * D :] = (values[:, 2 * D :] * valid).astype(BF16)
        pooled = nn(pool[...], joined[rows, :])
        for ref, lane in targets:
            start = STARTS[0] + first
            ref[start : start + POOL_CHUNK, :] = joined[rows, lane : lane + D]
            at = 0
            for level in range(1, LEVELS):
                count = POOL_CHUNK >> level
                part = pooled[at : at + count, lane : lane + D]
                at += count
                if ref is value:
                    part = part * float(1 << level)
                if level < LEVELS - 1:
                    start = STARTS[level] + chunk * count
                    ref[start : start + count, :] = part.astype(BF16)
                else:
                    top[chunk * count : chunk * count + count, lane : lane + D] = part
    for ref, lane in targets:
        ref[STARTS[-1] : STARTS[-1] + SIZES[-1], :] = top[:, lane : lane + D].astype(BF16)

    def score_step(rows, near, flat, kind):
        allowed = bias[kind]
        for pair in range(4):
            lanes = pair_lanes(pair)
            scores = nt(by_head(query[rows, lanes], half), key[near, lanes])
            probs[flat, lanes] = jnp.exp2(scores * SCORE + allowed).astype(BF16)

    window_loop(score_step)
    low_head = lax.broadcasted_iota(jnp.int32, (QUERIES, 128), 1) < DH

    def value_step(rows, near, flat, kind):
        number = counts[near, :]
        for pair in range(4):
            lanes = pair_lanes(pair)
            both = nn(probs[flat, lanes], jnp.concatenate([value[near, lanes], number], axis=1))
            numer[pair, rows, :] = joined_heads(both[:, :128], low_head)
            denom[pair, rows, :] = joined_heads(both[:, 128:], low_head)

    window_loop(value_step)
    spread_up(numer, 1.0)
    spread_up(denom, 1.0)

    def join_step(first):
        rows = pl.ds(first, 64)
        inner = pl.ds(STARTS[0] + first, 64)
        for pair in range(4):
            lanes = pair_lanes(pair)
            below = denom[pair, inner, :]
            attn[rows, lanes] = (numer[pair, inner, :] / below).astype(BF16)
            total[rows, lanes] = below

    row_loop(LEN, 64, join_step, 2)


def feed_kernel(
    plain,
    place,
    tokens,
    attn,
    total,
    cotangent,
    near_blocks,
    far_blocks,
    output,
    middle_grad,
    numer_grad,
    total_grad,
    near_grads,
    far_grads,
    w_out,
    w_up,
    w_down,
    vectors,
    middle,
    normed,
    inverse,
    normed_low,
    hidden,
    result,
    active,
    back,
    sums,
    acc_out,
    acc_up,
    acc_down,
):
    @pl.when(pl.program_id(0) == 0)
    def _():
        acc_out[...] = jnp.zeros_like(acc_out)
        acc_up[...] = jnp.zeros_like(acc_up)
        acc_down[...] = jnp.zeros_like(acc_down)
        sums[...] = jnp.zeros_like(sums)
        load_second(place, plain, (near_blocks, far_blocks), w_out, w_up, w_down, vectors)

    gain = vectors[0:1, :]
    shift = vectors[1:2, :]
    bias_down = vectors[2:3, :]
    middle[...] = nt(attn[...], w_out[...])

    def norm_step(first):
        rows = pl.ds(first, 64)
        values = middle[rows, :] + tokens[rows, :].astype(F32)
        middle[rows, :] = values
        norm, factor = layer_norm(values)
        normed[rows, :] = norm
        inverse[rows, :] = jnp.broadcast_to(factor, (64, 128))
        normed_low[rows, :] = (norm * gain + shift).astype(BF16)

    row_loop(LEN, 64, norm_step, 4)
    for part in range(FF // D):
        lanes = slice(D * part, D * part + D)
        hidden[...] = nt(normed_low[...], w_up[lanes, :])
        result[...] = nn(cotangent[...], w_down[:, lanes])
        bias_up = vectors[3 + part : 4 + part, :]

        def act_step(first, bias_up=bias_up, part=part):
            rows = pl.ds(first, 64)
            value = hidden[rows, :] + bias_up
            gate = 0.5 * jnp.tanh(0.5 * value) + 0.5
            active[rows, :] = (value * gate).astype(BF16)
            slope = gate * (1.0 + value * (1.0 - gate))
            gradient = (result[rows, :] * slope).astype(BF16)
            back[rows, :] = gradient
            at = 8 * (3 + part)
            sums[at : at + 8, :] += jnp.sum(gradient.astype(F32).reshape(8, 8, D), axis=0)

        row_loop(LEN, 64, act_step)
        acc_down[:, lanes] += tn(cotangent[...], active[...])
        acc_up[lanes, :] += tn(back[...], normed_low[...])
        middle[...] += nt(active[...], w_down[:, lanes])
        down = nn(back[...], w_up[lanes, :])
        gathered = down if part == 0 else gathered + down
    result[...] = gathered

    def back_step(first):
        rows = pl.ds(first, 64)
        output[rows, :] = (middle[rows, :] + bias_down).astype(BF16)
        gradient = result[rows, :]
        norm = normed[rows, :]
        value = cotangent[rows, :].astype(F32)
        sums[0:8, :] += jnp.sum((gradient * norm).reshape(8, 8, D), axis=0)
        sums[8:16, :] += jnp.sum(gradient.reshape(8, 8, D), axis=0)
        sums[16:24, :] += jnp.sum(value.reshape(8, 8, D), axis=0)
        value = value + norm_back(gradient, norm, inverse[rows, 0:1], gain)
        middle_grad[rows, :] = value.astype(BF16)

    row_loop(LEN, 64, back_step, 4)
    acc_out[...] += tn(middle_grad[...], attn[...])
    result[...] = nn(middle_grad[...], w_out[...])

    def numer_step(first):
        rows = pl.ds(first, 64)
        gradient = result[rows, :].astype(BF16).astype(F32) / total[rows, :]
        numer_grad[rows, :] = gradient.astype(BF16)
        total_grad[rows, :] = (-gradient * attn[rows, :].astype(F32)).astype(BF16)

    row_loop(LEN, 64, numer_step, 2)

    @pl.when(pl.program_id(0) == pl.num_programs(0) - 1)
    def _():
        small = jnp.sum(sums[...].reshape(7, 8, D), axis=1)
        small = jnp.concatenate([small, jnp.zeros((1, D), F32)], axis=0).astype(BF16)
        for half, block, device in block_places(place, plain, 1):
            target = (near_grads, far_grads)[half]
            target[block, 0:SHARE, :] = acc_out[sixteen(device), :].astype(BF16)
            target[block, SHARE : 5 * SHARE, :] = acc_up[sixty_four(device), :].astype(BF16)
            for part in range(4):
                at = (5 + part) * SHARE
                grads = acc_down[sixteen(device), D * part : D * part + D]
                target[block, at : at + SHARE, :] = grads.astype(BF16)
            target[block, 9 * SHARE : 9 * SHARE + 8, :] = small


def attend_back_kernel(
    plain,
    lengths,
    place,
    tokens,
    middle_grad,
    numer_grad,
    total_grad,
    query,
    key,
    value,
    probs,
    near_blocks,
    far_blocks,
    pool,
    half,
    grad_tokens,
    near_grads,
    far_grads,
    weights,
    vectors,
    numer,
    denom,
    score_grad,
    total,
    joined,
    normed,
    counts,
    top,
    sums,
    acc,
    result,
):
    step_index = pl.program_id(0)
    length = lengths[step_index]

    @pl.when(step_index == 0)
    def _():
        acc[...] = jnp.zeros_like(acc)
        sums[...] = jnp.zeros_like(sums)
        load_first(place, plain, (near_blocks, far_blocks), weights, vectors)

    gain = vectors[0:1, :]
    shift = vectors[1:2, :]
    clear_gaps(numer)
    clear_gaps(denom)
    fill_counts(counts, length)
    for source, target in ((numer_grad, numer), (total_grad, denom)):
        target[STARTS[0] : STARTS[0] + LEN, :] = source[...]
        for first in range(0, LEN, POOL_CHUNK):
            chunk = first // POOL_CHUNK
            pooled = nn(pool[...], source[first : first + POOL_CHUNK, :])
            at = 0
            for level in range(1, LEVELS):
                count = POOL_CHUNK >> level
                part = pooled[at : at + count] * float(1 << level)
                at += count
                if level < LEVELS - 1:
                    start = STARTS[level] + chunk * count
                    target[start : start + count, :] = part.astype(BF16)
                else:
                    top[chunk * count : chunk * count + count, :] = part
        target[STARTS[-1] : STARTS[-1] + SIZES[-1], :] = top[...].astype(BF16)

    def score_step(rows, near, flat, kind):
        number = counts[near, :]
        for pair in range(4):
            lanes = pair_lanes(pair)
            left = jnp.concatenate(
                [by_head(numer[rows, lanes], half), by_head(denom[rows, lanes], half)], axis=1
            )
            right = jnp.concatenate([value[near, lanes], number], axis=1)
            score_grad[flat, lanes] = (nt(left, right) * probs[flat, lanes].astype(F32)).astype(BF16)

    window_loop(score_step)
    low_head = lax.broadcasted_iota(jnp.int32, (QUERIES, 128), 1) < DH

    def query_step(rows, near, flat, kind):
        for pair in range(4):
            lanes = pair_lanes(pair)
            both = nn(score_grad[flat, lanes], key[near, lanes])
            total[pair, rows, :] = joined_heads(both, low_head)

    window_loop(query_step)
    spread_up(total, 0.5)

    def take(at, scale, masked):
        def take_step(first):
            rows = pl.ds(first, 64)
            if masked:
                place = lax.broadcasted_iota(jnp.int32, (64, 1), 0) + first
                valid = (place < length).astype(F32)
            for pair in range(4):
                values = total[pair, pl.ds(STARTS[0] + first, 64), :]
                if scale != 1.0:
                    values = values * scale
                if masked:
                    values = values * valid
                joined[rows, at + 128 * pair : at + 128 * pair + 128] = values.astype(BF16)

        row_loop(LEN, 64, take_step, 2)

    take(0, 0.125, False)
    for at, left, right, factor, scale, masked in (
        (D, score_grad, query, 0.5, 0.125, False),
        (2 * D, probs, numer, 1.0, 1.0, True),
    ):
        total[...] = jnp.zeros_like(total)

        def near_step(rows, near, flat, kind, left=left, right=right):
            for pair in range(4):
                lanes = pair_lanes(pair)
                total[pair, near, :] += tn(left[flat, lanes], by_head(right[rows, lanes], half))

        window_loop(near_step)
        spread_up(total, factor)
        take(at, scale, masked)

    def norm_step(first):
        rows = pl.ds(first, 64)
        values, _ = layer_norm(tokens[rows, :].astype(F32))
        normed[rows, :] = (values * gain + shift).astype(BF16)

    row_loop(LEN, 64, norm_step, 4)
    acc[...] += tn(joined[...], normed[...])
    result[...] = nn(joined[...], weights[...])

    def back_step(first):
        rows = pl.ds(first, 64)
        norm, inverse = layer_norm(tokens[rows, :].astype(F32))
        gradient = result[rows, :]
        sums[0:8, :] += jnp.sum((gradient * norm).reshape(8, 8, D), axis=0)
        sums[8:16, :] += jnp.sum(gradient.reshape(8, 8, D), axis=0)
        value = middle_grad[rows, :].astype(F32) + norm_back(gradient, norm, inverse, gain)
        grad_tokens[rows, :] = value.astype(BF16)

    row_loop(LEN, 64, back_step, 4)

    @pl.when(step_index == pl.num_programs(0) - 1)
    def _():
        small = jnp.sum(sums[...].reshape(2, 8, D), axis=1)
        small = jnp.concatenate([small, jnp.zeros((6, D), F32)], axis=0).astype(BF16)
        for side, block, device in block_places(place, plain, 1):
            target = (near_grads, far_grads)[side]
            for part in range(3):
                rows = pl.ds(pl.multiple_of(part * D + device * SHARE, SHARE), SHARE)
                target[block, part * SHARE : part * SHARE + SHARE, :] = acc[rows, :].astype(BF16)
            target[block, 3 * SHARE : 3 * SHARE + 8, :] = small


SMEM = pl.BlockSpec(memory_space=pltpu.SMEM)


def whole(*shape):
    return pl.BlockSpec(shape, lambda i: (0,) * len(shape), pipeline_mode=pl.Buffered(1))


def per_sequence(rows, columns):
    return pl.BlockSpec((rows, columns), lambda i: (i, 0))


def vmem(rows, columns, dtype):
    return pltpu.VMEM((rows, columns), dtype)


def shape_of(rows, columns, dtype):
    return jax.ShapeDtypeStruct((rows, columns), dtype)


PARAMS = pltpu.CompilerParams(
    dimension_semantics=("arbitrary",), vmem_limit_bytes=63 * 1024 * 1024
)


def cost(microseconds):
    return pl.CostEstimate(
        flops=int(microseconds * 1.0e9), bytes_accessed=int(microseconds * 1.0e6), transcendentals=0
    )


def attend(lengths, place, plain, tokens, blocks):
    count = lengths.shape[0]
    levels = shape_of(count * ROWS, D, BF16)
    one = per_sequence(LEN, D)
    all_levels = per_sequence(ROWS, D)
    flat = WINDOWS * 2 * QUERIES
    return pl.pallas_call(
        functools.partial(attend_kernel, plain),
        grid=(count,),
        in_specs=[
            SMEM,
            SMEM,
            one,
            whole(16, FIRST_ROWS, D),
            whole(16, FIRST_ROWS, D),
            whole(2, 2 * QUERIES, KEYS),
            whole(POOL_CHUNK, POOL_CHUNK),
            whole(2, 128),
        ],
        out_specs=[all_levels] * 3 + [per_sequence(flat, D), one, one],
        out_shape=[levels] * 3
        + [
            shape_of(count * flat, D, BF16),
            shape_of(count * LEN, D, BF16),
            shape_of(count * LEN, D, F32),
        ],
        scratch_shapes=[
            vmem(3 * D, D, BF16),
            vmem(8, D, F32),
            vmem(LEN, D, BF16),
            vmem(LEN, 3 * D, BF16),
            vmem(SIZES[-1], 3 * D, F32),
            vmem(ROWS, 128, BF16),
            pltpu.VMEM((4, ROWS, 128), F32),
            pltpu.VMEM((4, ROWS, 128), F32),
        ],
        compiler_params=PARAMS,
        cost_estimate=cost(40),
        name="attend",
    )(
        lengths,
        place,
        tokens,
        *blocks,
        jnp.asarray(score_bias()),
        jnp.asarray(pool_matrix(), BF16),
        jnp.asarray(halves(), BF16),
    )


def feed(place, plain, tokens, attn, total, cotangent, blocks):
    rows = tokens.shape[0]
    one = per_sequence(LEN, D)
    low = shape_of(rows, D, BF16)
    grads = whole(16, SECOND_ROWS, D)
    return pl.pallas_call(
        functools.partial(feed_kernel, plain),
        grid=(rows // LEN,),
        in_specs=[SMEM] + [one] * 4 + [whole(16, SECOND_ROWS, D)] * 2,
        out_specs=[one] * 4 + [grads, grads],
        out_shape=[low] * 4 + [jax.ShapeDtypeStruct((16, SECOND_ROWS, D), BF16)] * 2,
        scratch_shapes=[
            vmem(D, D, BF16),
            vmem(FF, D, BF16),
            vmem(D, FF, BF16),
            vmem(8, D, F32),
            vmem(LEN, D, F32),
            vmem(LEN, D, F32),
            vmem(LEN, 128, F32),
            vmem(LEN, D, BF16),
            vmem(LEN, D, F32),
            vmem(LEN, D, F32),
            vmem(LEN, D, BF16),
            vmem(LEN, D, BF16),
            vmem(56, D, F32),
            vmem(D, D, F32),
            vmem(FF, D, F32),
            vmem(D, FF, F32),
        ],
        compiler_params=PARAMS,
        cost_estimate=cost(75),
        name="feed",
    )(place, tokens, attn, total, cotangent, *blocks)


def attend_back(lengths, place, plain, tokens, middle_grad, numer_grad, total_grad, kept, blocks):
    count = lengths.shape[0]
    one = per_sequence(LEN, D)
    all_levels = per_sequence(ROWS, D)
    flat = WINDOWS * 2 * QUERIES
    grads = whole(16, FIRST_ROWS, D)
    return pl.pallas_call(
        functools.partial(attend_back_kernel, plain),
        grid=(count,),
        in_specs=[SMEM, SMEM]
        + [one] * 4
        + [all_levels] * 3
        + [per_sequence(flat, D)]
        + [whole(16, FIRST_ROWS, D)] * 2
        + [whole(POOL_CHUNK, POOL_CHUNK), whole(2, 128)],
        out_specs=[one, grads, grads],
        out_shape=[shape_of(count * LEN, D, BF16)]
        + [jax.ShapeDtypeStruct((16, FIRST_ROWS, D), BF16)] * 2,
        scratch_shapes=[
            vmem(3 * D, D, BF16),
            vmem(8, D, F32),
            vmem(ROWS, D, BF16),
            vmem(ROWS, D, BF16),
            vmem(flat, D, BF16),
            pltpu.VMEM((4, ROWS, 128), F32),
            vmem(LEN, 3 * D, BF16),
            vmem(LEN, D, BF16),
            vmem(ROWS, 128, BF16),
            vmem(SIZES[-1], D, F32),
            vmem(16, D, F32),
            vmem(3 * D, D, F32),
            vmem(LEN, D, F32),
        ],
        compiler_params=PARAMS,
        cost_estimate=cost(60),
        name="attend_back",
    )(
        lengths,
        place,
        tokens,
        middle_grad,
        numer_grad,
        total_grad,
        *kept,
        *blocks,
        jnp.asarray(pool_matrix(), BF16),
        jnp.asarray(halves(), BF16),
    )


def pack_first_kernel(place, w_query, w_key, w_value, small, packed):
    for part, ref in enumerate((w_query, w_key, w_value)):
        packed[part * SHARE : part * SHARE + SHARE, :] = ref[...].astype(F32).T.astype(BF16)
    device = place[0] * 8 + place[1]
    lane = lax.broadcasted_iota(jnp.int32, (SHARE, D), 1)
    mine = lane == lax.broadcasted_iota(jnp.int32, (SHARE, D), 0) + device * SHARE
    packed[3 * SHARE :, :] = nn(small[...], mine.astype(F32).astype(BF16)).astype(BF16)


def pack_second_kernel(place, w_out, w_up, w_down, small, bias_up, packed):
    packed[0:SHARE, :] = w_out[...].astype(F32).T.astype(BF16)
    packed[SHARE : 5 * SHARE, :] = w_up[...].astype(F32).T.astype(BF16)
    for part in range(4):
        at = (5 + part) * SHARE
        rows = slice(D * part, D * part + D)
        packed[at : at + SHARE, :] = w_down[rows, :].astype(F32).T.astype(BF16)
    device = place[0] * 8 + place[1]
    lane = lax.broadcasted_iota(jnp.int32, (SHARE, D), 1)
    mine = lane == lax.broadcasted_iota(jnp.int32, (SHARE, D), 0) + device * SHARE
    vectors = nn(small[...], mine.astype(F32).astype(BF16))
    lane = lax.broadcasted_iota(jnp.int32, (4 * SHARE, D), 1)
    mine = lane == lax.broadcasted_iota(jnp.int32, (4 * SHARE, D), 0) + (device % 8) * 4 * SHARE
    wide = nn(bias_up[...], mine.astype(F32).astype(BF16))
    row = lax.broadcasted_iota(jnp.int32, (8, D), 0)
    vectors = vectors + jnp.where(row == 3 + device // 8, wide, 0.0)
    packed[9 * SHARE :, :] = vectors.astype(BF16)


def pack(kernel, rows, name, place, *operands):
    return pl.pallas_call(
        kernel,
        in_specs=[SMEM] + [pl.BlockSpec(memory_space=pltpu.VMEM)] * len(operands),
        out_specs=pl.BlockSpec(memory_space=pltpu.VMEM),
        out_shape=shape_of(rows, D, BF16),
        cost_estimate=cost(2),
        name=name,
    )(place, *operands)


def across(values, bits):
    return lax.ppermute(values, "fsdp", [(i, i ^ bits) for i in range(8)])


def along(values, step):
    return lax.ppermute(values, "dp", [(i, (i + step) % 4) for i in range(4)])


def gather_rows(packed):
    return jnp.stack([packed] + [along(packed, step) for step in (1, 2, 3)])


def scatter_rows(blocks):
    parts = [blocks[0]] + [along(blocks[step], step) for step in (1, 2, 3)]
    return sum(part.astype(F32) for part in parts)


def spread(vector, index, devices):
    share = vector.shape[0]
    full = jnp.tile(vector, devices)
    mine = lax.broadcasted_iota(jnp.int32, full.shape, 0) // share == index
    return jnp.where(mine, full, jnp.zeros_like(full)).reshape(-1, D)


def stack_vectors(vectors):
    rows = jnp.stack(vectors)
    return jnp.concatenate([rows, jnp.zeros((8 - len(vectors), rows.shape[1]), rows.dtype)])


def exchange_permutes(place, tokens, lengths, weights, vectors, cotangent):
    w_query, w_key, w_value, w_out, w_up, w_down = weights
    bias_up, bias_down, gain_attn, shift_attn, gain_ffn, shift_ffn = vectors
    small = stack_vectors([gain_attn, shift_attn])
    first = pack(pack_first_kernel, FIRST_ROWS, "pack_first", place, w_query, w_key, w_value, small)
    small = stack_vectors([gain_ffn, shift_ffn, bias_down])
    second = pack(
        pack_second_kernel,
        SECOND_ROWS,
        "pack_second",
        place,
        w_out,
        w_up,
        w_down,
        small,
        bias_up.reshape(1, -1),
    )
    rows = gather_rows(first)
    in_x, in_y = across(rows, 2), across(rows, 4)
    diagonal = jnp.concatenate([across(in_x[:2], 4), across(in_y[2:], 2)])
    near = jnp.concatenate([rows, in_x, in_y, diagonal])
    first_blocks = (near, across(near, 1))
    second_rows = gather_rows(second)
    others = [across(second_rows, bits) for bits in (2, 4, 6)]
    *kept, attn, total = attend(lengths, place, False, tokens, first_blocks)
    near = jnp.concatenate([second_rows] + others)
    second_blocks = (near, across(near, 1))
    output, middle_grad, numer_grad, total_grad, near, far = feed(
        place, False, tokens, attn, total, cotangent, second_blocks
    )
    mine = (near.astype(F32) + across(far, 1).astype(F32)).astype(BF16).reshape(4, 4, SECOND_ROWS, D)
    others = [across(mine[block], bits) for block, bits in ((1, 2), (2, 4), (3, 6))]
    grad_tokens, near, far = attend_back(
        lengths, place, False, tokens, middle_grad, numer_grad, total_grad, kept, first_blocks
    )
    mine = sum(part.astype(F32) for part in [mine[0]] + others).astype(BF16)
    second_share = scatter_rows(mine)
    mine = (near.astype(F32) + across(far, 1).astype(F32)).astype(BF16).reshape(4, 4, FIRST_ROWS, D)
    mine = (mine[:2].astype(F32) + across(mine[2:], 4).astype(F32)).astype(BF16)
    mine = (mine[0].astype(F32) + across(mine[1], 2).astype(F32)).astype(BF16)
    first_share = scatter_rows(mine)
    return output, grad_tokens, first_share, second_share


def exchange_plain(index, devices, tokens, lengths, weights, vectors, cotangent):
    w_query, w_key, w_value, w_out, w_up, w_down = weights
    bias_up, bias_down, gain_attn, shift_attn, gain_ffn, shift_ffn = vectors
    share = D // devices

    def gathered(rows):
        return lax.all_gather(rows, AXES, axis=0, tiled=True).reshape(32, SHARE, D)

    def vector_rows(parts):
        rows = jnp.concatenate([spread(part, index, devices) for part in parts])
        rows = lax.psum(rows, AXES)
        pad = jnp.zeros((8 - rows.shape[0], D), rows.dtype)
        rows = jnp.concatenate([rows, pad])[None]
        return jnp.concatenate([rows, jnp.zeros((31, 8, D), rows.dtype)])

    def halved(parts):
        blocks = jnp.concatenate(parts, axis=1)
        return blocks[:16], blocks[16:]

    place = jnp.zeros((2,), jnp.int32)
    first_blocks = halved(
        [gathered(w.T) for w in (w_query, w_key, w_value)]
        + [vector_rows([gain_attn, shift_attn])]
    )
    up = lax.all_gather(w_up.T, AXES, axis=0, tiled=True).reshape(32, 4 * SHARE, D)
    down = lax.all_gather(w_down.T, AXES, axis=0, tiled=True).reshape(32, SHARE, 4, D)
    down = jnp.transpose(down, (0, 2, 1, 3)).reshape(32, 4 * SHARE, D)
    second_blocks = halved(
        [gathered(w_out.T), up, down, vector_rows([gain_ffn, shift_ffn, bias_down, bias_up])]
    )
    *kept, attn, total = attend(lengths, place, True, tokens, first_blocks)
    output, middle_grad, numer_grad, total_grad, near, far = feed(
        place, True, tokens, attn, total, cotangent, second_blocks
    )
    second = jnp.concatenate([near, far])
    grad_tokens, near, far = attend_back(
        lengths, place, True, tokens, middle_grad, numer_grad, total_grad, kept, first_blocks
    )
    first = jnp.concatenate([near, far])

    def scattered(rows):
        rows = rows.reshape(devices, -1, D)
        return lax.psum_scatter(rows, AXES, scatter_dimension=0, tiled=False).astype(F32)

    down = second[:, 5 * SHARE : 9 * SHARE].reshape(32, 4, SHARE, D)
    down = scattered(jnp.transpose(down, (0, 2, 1, 3)).reshape(32, 4 * SHARE, D))
    down = jnp.transpose(down.reshape(share, 4, D), (1, 0, 2)).reshape(4 * share, D)
    first_vectors = lax.psum(first[0, 3 * SHARE :].astype(F32), AXES)
    second_vectors = lax.psum(second[0, 9 * SHARE :].astype(F32), AXES)
    first_share = [scattered(first[:, p * SHARE : p * SHARE + SHARE]) for p in range(3)]
    second_share = [scattered(second[:, :SHARE]), scattered(second[:, SHARE : 5 * SHARE]), down]
    return (
        output,
        grad_tokens,
        jnp.concatenate(first_share + [first_vectors]),
        jnp.concatenate(second_share + [second_vectors]),
    )


def on_device(sizes, tokens, lengths, *rest):
    weights, vectors, cotangent = rest[:6], rest[6:12], rest[12]
    devices = sizes[0] * sizes[1]
    share = D // devices
    index = lax.axis_index(AXES)
    if sizes == (4, 8):
        place = jnp.stack([lax.axis_index("dp"), lax.axis_index("fsdp")]).astype(jnp.int32)
        output, grad_tokens, first, second = exchange_permutes(
            place, tokens, lengths, weights, vectors, cotangent
        )
    else:
        output, grad_tokens, first, second = exchange_plain(
            index, devices, tokens, lengths, weights, vectors, cotangent
        )

    def own(row):
        return lax.dynamic_slice(row, (index * share,), (share,))

    first_vectors = first[3 * share :]
    second_vectors = second[9 * share :]
    down = jnp.transpose(second[5 * share : 9 * share].reshape(4, share, D), (0, 2, 1))
    return (
        output,
        grad_tokens,
        first[:share].T,
        first[share : 2 * share].T,
        first[2 * share : 3 * share].T,
        second[:share].T,
        second[share : 5 * share].T,
        down.reshape(FF, share),
        lax.dynamic_slice(second_vectors[3:7].reshape(FF), (index * 4 * share,), (4 * share,)),
        own(second_vectors[2]),
        own(first_vectors[0]),
        own(first_vectors[1]),
        own(second_vectors[0]),
        own(second_vectors[1]),
    )


def solution(mesh):
    rows = P(AXES, None)
    columns = P(None, AXES)
    vector = P(AXES)
    sizes = (mesh.shape["dp"], mesh.shape["fsdp"])
    return jax.shard_map(
        functools.partial(on_device, sizes),
        mesh=mesh,
        in_specs=(rows, vector) + (columns,) * 6 + (vector,) * 6 + (rows,),
        out_specs=(rows, rows) + (columns,) * 6 + (vector,) * 6,
        check_vma=False,
    )
```

time: 1910 us -> 341 us (0.18)
  local copies, waits for them, and re-layouts: 570 us -> 20.6 us
  waiting for transfers between devices: 465 us -> 79.3 us
  matrix products: 360 us -> 0 us
  blocking collectives: 244 us -> 0 us
  other arithmetic: 240 us -> 8.72 us
  Pallas kernels: 0 us -> 194 us
  starting transfers between devices: 0.5 us -> 37.1 us
    reduce_scatter x6 -> x0, waiting for transfers between devices: 463 us -> none  [the longest x1 140 us: on_device(): lax.psum_scatter(grad_down, ('dp', 'fsdp'), scatter_dimension=1, tiled=True)]
    dot_general x54 -> x0, matrix products: 360 us -> none  [the longest x6 51.3 us: rdot(): lax.dot_general(left, right, (((1,), (1,)), ((), ())), preferred_element_...]
    pallas_call x0 -> x5, Pallas kernels: none -> 194 us  [the longest x1 80.8 us: feed(): pl.pallas_call(functools.partial(feed_kernel, plain), grid=(rows // LEN,)...]
    all_gather x4 -> x0, blocking collectives: 164 us -> none  [the longest x1 45.4 us: on_device(): lax.all_gather(w_query, ('dp', 'fsdp'), axis=1, tiled=True)]
    reshape x44 -> x1, local copies, waits for them, and re-layouts: 129 us -> 0.66 us  [on_device(): down.reshape(FF, share)]
    slice x50 -> x7, local copies, waits for them, and re-layouts: 112 us -> 2.01 us  [the longest x1 1.25 us: exchange_permutes(): mine[block]]
    add x41 -> x2, other arithmetic: 81.6 us -> 0.94 us  [scatter_rows(): return sum((part.astype(F32) for part in parts))]
    unnamed x2 -> x0, blocking collectives: 79.5 us -> none
  transfers between devices with their start and end apart: 8 -> 28, of which waited for: 4 -> 14; matrix products, arithmetic and copies ran while one was open for 49% -> 4% of each run, Pallas kernels for 0% -> 13%
where the time goes in v1:
time: 341 us
  Pallas kernels  194 us (57%)
  waiting for transfers between devices  79.3 us (23%)
  starting transfers between devices  37.1 us (11%)
  local copies, waits for them, and re-layouts  20.6 us (6%)
  other arithmetic  8.72 us (3%)
    pallas_call x1, Pallas kernels, feed(): pl.pallas_call(functools.partial(feed_kernel, plain), grid=(rows // LEN,)...  80.8 us
    pallas_call x1, Pallas kernels, attend_back(): pl.pallas_call(functools.partial(attend_back_kernel, plain), grid=(count,...  66.5 us
    ppermute x16, waiting for transfers between devices, across(): return lax.ppermute(values, 'fsdp', [(i, i ^ bits) for i in range(8)])  56 us
    pallas_call x1, Pallas kernels, attend(): pl.pallas_call(functools.partial(attend_kernel, plain), grid=(count,), in...  42.5 us
    ppermute x12, waiting for transfers between devices, along(): return lax.ppermute(values, 'dp', [(i, (i + step) % 4) for i in range(4)])  23.3 us
    ppermute x12, starting transfers between devices, along(): return lax.ppermute(values, 'dp', [(i, (i + step) % 4) for i in range(4)])  19.8 us
    ppermute x16, starting transfers between devices, across(): return lax.ppermute(values, 'fsdp', [(i, i ^ bits) for i in range(8)])  17.4 us
    unnamed x39, local copies, waits for them, and re-layouts  12.6 us
  transfers between devices with their start and end apart: 28, of which 14 were waited for; matrix products, arithmetic and copies ran while one was open for 4% of the time, Pallas kernels for 13%

profile of v1, /device:TPU:0, one launch (start us, length us, event | category | flops | bytes accessed | tf_op | source)
XLA Modules:
  0.0 340.5 jit_solution(2307630159843790658)
XLA Ops:
  0.7 1.5 copy.34.w_query
  2.1 1.5 copy.35.w_key
  3.6 1.5 copy.36.w_value
  5.7 1.3 maximum_maximum_fusion.small
  7.1 1.9 pack_first.1
  9.0 5.0 %collective-permute-start.2 = (bf16[56,512]{1,0:T(8,128)(2,1)}, bf16[56,512]{1,0:T(8,128)(2,1)S(1)}, u32[]{:S(2)}, u32[]{:S(2)}) collective-permute-start(bf16[56,512]{1,0:T(8,128)(2,1)} %pack_first.1), channel_id=1, source_target_pairs={{0,24},{8,0},{16,8},{24,16},{1,25},{9,1},{17,9},{25,17},{2,26},{10... | collective-permute-start | bytes 172040 | tf_op jit(solution)/shard_map/ppermute | solution.py:786
  14.0 1.0 collective-permute-start
  15.1 0.8 copy.37.w_out
  15.9 0.8 copy.38.w_up
  16.7 1.0 copy.39.w_down
  17.7 0.7 maximum_maximum_fusion.1.small
  18.3 2.1 pack_second.1
  20.5 2.8 collective-permute-start.10
  23.3 1.1 collective-permute-start.9
  24.4 1.6 constant_dynamic-update-slice_fusion.14
  26.2 1.6 collective-permute-start.4
  27.8 1.5 collective-permute-start.3
  29.3 8.2 %collective-permute-done.9 = bf16[152,512]{1,0:T(8,128)(2,1)S(1)} collective-permute-done((bf16[152,512]{1,0:T(8,128)(2,1)}, bf16[152,512]{1,0:T(8,128)(2,1)S(1)}, u32[]{:S(2)}, u32[]{:S(2)}) %collective-permute-start.9) | collective-permute-done | bytes 155680 | tf_op jit(solution)/shard_map/ppermute | solution.py:786
  37.5 1.0 pad_maximum_fusion
  38.5 2.5 collective-permute-start.13
  42.1 1.6 collective-permute-start.6
  43.7 1.6 collective-permute-start.5
  45.3 24.0 %collective-permute-done.5 = bf16[2,56,512]{2,1,0:T(8,128)(2,1)S(1)} collective-permute-done((bf16[2,56,512]{2,1,0:T(8,128)(2,1)S(1)}, bf16[2,56,512]{2,1,0:T(8,128)(2,1)S(1)}, u32[]{:S(2)}, u32[]{:S(2)}) %collective-permute-start.5) | collective-permute-done | bytes 114720 | tf_op jit(solution)/shard_map/ppermute | solution.py:782
  69.5 0.8 constant_dynamic-update-slice_fusion.13
  70.3 0.7 constant_dynamic-update-slice_fusion.12
  71.0 0.7 constant_dynamic-update-slice_fusion.11
  71.7 0.9 constant_dynamic-update-slice_fusion.10
  72.6 0.9 constant_dynamic-update-slice_fusion.9
  73.5 0.9 constant_dynamic-update-slice_fusion.8.near_blocks
  74.8 42.5 %attend.1 = (bf16[6576,512]{1,0:T(8,128)(2,1)}, bf16[6576,512]{1,0:T(8,128)(2,1)}, bf16[6576,512]{1,0:T(8,128)(2,1)}, bf16[12288,512]{1,0:T(8,128)(2,1)}, bf16[3...) custom-call(s32[3]{0:T(128)} %lengths.3, s32[2]{0:T(128)} %pad_add_fusion.place, bf16[3072,512]{1,0:T(8,128)(2,1)} %tokens.5, ...), custom_call_target="tpu_custom_call" | custom-call | flops 40000000000 | bytes 40000000 | tf_op jit(solution)/shard_map/attend/pallas_call | solution.py:613
  117.3 80.8 %feed.1 = (bf16[3072,512]{1,0:T(8,128)(2,1)}, bf16[3072,512]{1,0:T(8,128)(2,1)}, bf16[3072,512]{1,0:T(8,128)(2,1)}, bf16[3072,512]{1,0:T(8,128)(2,1)}, bf16[16,1...) custom-call(s32[2]{0:T(128)} %pad_add_fusion.place, bf16[3072,512]{1,0:T(8,128)(2,1)} %tokens.5, ...), custom_call_target="tpu_custom_call" | custom-call | flops 74999996416 | bytes 75000000 | tf_op jit(solution)/shard_map/feed/pallas_call | solution.py:662
  198.1 66.5 %attend_back.1 = (bf16[3072,512]{1,0:T(8,128)(2,1)}, bf16[16,56,512]{2,1,0:T(8,128)(2,1)}, bf16[16,56,512]{2,1,0:T(8,128)(2,1)}) custom-call(s32[3]{0:T(128)} %lengths.3, s32[2]{0:T(128)} %pad_add_fusion.place, bf16[3072,512]{1,0:T(8,128)(2,1)} %tokens.5, bf16[3072,512]{1,0:T(8,128)(2,1)} %get-tuple-element.32.middle_grad, ...), custom_call_target="tpu_custom_call" | custom-call | flops 60000002048 | bytes 60000000 | tf_op jit(solution)/shard_map/attend_back/pallas_call | solution.py:698
  265.2 2.2 collective-permute-done.15
  267.3 1.4 add_convert_fusion.1
  268.9 1.5 collective-permute-start.16
  270.4 11.1 %collective-permute-done.16 = bf16[2,4,56,512]{3,2,1,0:T(8,128)(2,1)S(1)} collective-permute-done((bf16[2,4,56,512]{3,2,1,0:T(8,128)(2,1)S(1)}, bf16[2,4,56,512]{3,2,1,0:T(8,128)(2,1)S(1)}, u32[]{:S(2)}, u32[]{:S(2)}) %collective-permute-start.16) | collective-permute-done | bytes 458784 | tf_op jit(solution)/shard_map/ppermute | solution.py:782
  281.6 1.6 collective-permute-start.17
  283.2 5.3 %collective-permute-done.17 = bf16[4,56,512]{2,1,0:T(8,128)(2,1)S(1)} collective-permute-done((bf16[4,56,512]{2,1,0:T(8,128)(2,1)S(1)}, bf16[4,56,512]{2,1,0:T(8,128)(2,1)S(1)}, u32[]{:S(2)}, u32[]{:S(2)}) %collective-permute-start.17) | collective-permute-done | bytes 229408 | tf_op jit(solution)/shard_map/ppermute | solution.py:782
  288.6 0.8 add_convert_fusion
  289.4 1.2 fusion.11
  290.7 1.5 collective-permute-start.22
  292.2 1.4 collective-permute-start.24
  294.2 0.6 slice_bitcast_fusion.9
  294.8 0.9 collective-permute-start.18
  295.7 3.0 collective-permute-start.20
  298.6 2.3 collective-permute-done.18
  300.9 1.1 collective-permute-start.19
  302.0 4.1 %collective-permute-done.19 = bf16[56,512]{1,0:T(8,128)(2,1)} collective-permute-done((bf16[56,512]{1,0:T(8,128)(2,1)S(1)}, bf16[56,512]{1,0:T(8,128)(2,1)}, u32[]{:S(2)}, u32[]{:S(2)}) %collective-permute-start.19) | collective-permute-done | bytes 57376 | tf_op jit(solution)/shard_map/ppermute | solution.py:786
  306.1 0.9 fusion.5
  306.9 0.6 slice_bitcast_fusion.12
  307.9 11.7 %collective-permute-done.24 = bf16[4,152,512]{2,1,0:T(8,128)(2,1)} collective-permute-done((bf16[4,152,512]{2,1,0:T(8,128)(2,1)}, bf16[4,152,512]{2,1,0:T(8,128)(2,1)}, u32[]{:S(2)}, u32[]{:S(2)}) %collective-permute-start.24) | collective-permute-done | bytes 622624 | tf_op jit(solution)/shard_map/ppermute | solution.py:782
  319.6 1.2 collective-permute-done.23
  320.8 1.8 add_convert_fusion.2
  322.6 0.9 collective-permute-start.25
  323.5 3.0 collective-permute-start.27
  326.5 0.9 collective-permute-start.26
  327.4 0.6 fusion.7
  328.0 2.2 collective-permute-done.25
  330.2 1.3 collective-permute-done.27
  331.5 5.2 %collective-permute-done.26 = bf16[152,512]{1,0:T(8,128)(2,1)S(1)} collective-permute-done((bf16[152,512]{1,0:T(8,128)(2,1)S(1)}, bf16[152,512]{1,0:T(8,128)(2,1)S(1)}, u32[]{:S(2)}, u32[]{:S(2)}) %collective-permute-start.26) | collective-permute-done | bytes 155680 | tf_op jit(solution)/shard_map/ppermute | solution.py:786
  336.8 0.6 slice_bitcast_fusion.11
  337.4 0.7 fusion.14
  338.7 0.7 copy.41
  339.3 0.6 fusion.6
  (71 shorter events, 5.7 us)
Async XLA Ops:
  7.1 8.1 %copy-start.4 = (bf16[512,16]{0,1:T(8,128)(2,1)S(1)}, bf16[512,16]{0,1:T(8,128)(2,1)}, u32[]{:S(2)}) copy-start(bf16[512,16]{0,1:T(8,128)(2,1)} %param.25) | copy-start | bytes 49156
  7.1 8.8 %copy-start.2 = (bf16[512,64]{0,1:T(8,128)(2,1)S(1)}, bf16[512,64]{0,1:T(8,128)(2,1)}, u32[]{:S(2)}) copy-start(bf16[512,64]{0,1:T(8,128)(2,1)} %param.26) | copy-start | bytes 196612
  7.1 9.6 %copy-start.3 = (bf16[2048,16]{0,1:T(8,128)(2,1)S(1)}, bf16[2048,16]{0,1:T(8,128)(2,1)}, u32[]{:S(2)}) copy-start(bf16[2048,16]{0,1:T(8,128)(2,1)} %param.27) | copy-start | bytes 196612
  7.1 10.6 %copy-start.6 = (bf16[16]{0:T(256)(128)(2,1)S(1)}, bf16[16]{0:T(256)(128)(2,1)}, u32[]{:S(2)}) copy-start(bf16[16]{0:T(256)(128)(2,1)} %param.29) | copy-start | bytes 100
  7.1 10.6 %copy-start.7 = (bf16[16]{0:T(256)(128)(2,1)S(1)}, bf16[16]{0:T(256)(128)(2,1)}, u32[]{:S(2)}) copy-start(bf16[16]{0:T(256)(128)(2,1)} %param.33) | copy-start | bytes 100
  7.1 10.6 %copy-start.8 = (bf16[16]{0:T(256)(128)(2,1)S(1)}, bf16[16]{0:T(256)(128)(2,1)}, u32[]{:S(2)}) copy-start(bf16[16]{0:T(256)(128)(2,1)} %param.32) | copy-start | bytes 100
  9.0 17.0 %collective-permute-start.2 = (bf16[56,512]{1,0:T(8,128)(2,1)}, bf16[56,512]{1,0:T(8,128)(2,1)S(1)}, u32[]{:S(2)}, u32[]{:S(2)}) collective-permute-start(bf16[56,512]{1,0:T(8,128)(2,1)} %pack_first.1), channel_id=1, source_target_pairs={{0,24},{8,0},{16,8},{24,16},{1,25},{9,1},{17,9},{25,17},{2,26},{10... | collective-permute-start | bytes 172040 | tf_op jit(solution)/shard_map/ppermute | solution.py:786
  14.0 12.1 %collective-permute-start.1 = (bf16[56,512]{1,0:T(8,128)(2,1)}, bf16[56,512]{1,0:T(8,128)(2,1)S(1)}, u32[]{:S(2)}, u32[]{:S(2)}) collective-permute-start(bf16[56,512]{1,0:T(8,128)(2,1)} %pack_first.1), channel_id=1, source_target_pairs={{0,16},{8,24},{16,0},{24,8},{1,17},{9,25},{17,1},{25,9},{2,18},{10... | collective-permute-start | bytes 172040 | tf_op jit(solution)/shard_map/ppermute | solution.py:786
  14.0 12.1 %collective-permute-start = (bf16[56,512]{1,0:T(8,128)(2,1)}, bf16[56,512]{1,0:T(8,128)(2,1)S(1)}, u32[]{:S(2)}, u32[]{:S(2)}) collective-permute-start(bf16[56,512]{1,0:T(8,128)(2,1)} %pack_first.1), channel_id=1, source_target_pairs={{0,8},{8,16},{16,24},{24,0},{1,9},{9,17},{17,25},{25,1},{2,10},{10... | collective-permute-start | bytes 172040 | tf_op jit(solution)/shard_map/ppermute | solution.py:786
  18.3 7.7 %copy-start.1 = (bf16[56,512]{1,0:T(8,128)(2,1)S(1)}, bf16[56,512]{1,0:T(8,128)(2,1)}, u32[]{:S(2)}) copy-start(bf16[56,512]{1,0:T(8,128)(2,1)} %pack_first.1) | copy-start | bytes 172036
  20.5 8.8 %collective-permute-start.10 = (bf16[152,512]{1,0:T(8,128)(2,1)}, bf16[152,512]{1,0:T(8,128)(2,1)S(1)}, u32[]{:S(2)}, u32[]{:S(2)}) collective-permute-start(bf16[152,512]{1,0:T(8,128)(2,1)} %pack_second.1), channel_id=1, source_target_pairs={{0,24},{8,0},{16,8},{24,16},{1,25},{9,1},{17,9},{25,17},{2,26},{10... | collective-permute-start | bytes 466952 | tf_op jit(solution)/shard_map/ppermute | solution.py:786
  23.3 14.2 %collective-permute-start.9 = (bf16[152,512]{1,0:T(8,128)(2,1)}, bf16[152,512]{1,0:T(8,128)(2,1)S(1)}, u32[]{:S(2)}, u32[]{:S(2)}) collective-permute-start(bf16[152,512]{1,0:T(8,128)(2,1)} %pack_second.1), channel_id=1, source_target_pairs={{0,16},{8,24},{16,0},{24,8},{1,17},{9,25},{17,1},{25,9},{2,18},{10... | collective-permute-start | bytes 466952 | tf_op jit(solution)/shard_map/ppermute | solution.py:786
  26.0 11.5 %collective-permute-start.8 = (bf16[152,512]{1,0:T(8,128)(2,1)}, bf16[152,512]{1,0:T(8,128)(2,1)S(1)}, u32[]{:S(2)}, u32[]{:S(2)}) collective-permute-start(bf16[152,512]{1,0:T(8,128)(2,1)} %pack_second.1), channel_id=1, source_target_pairs={{0,8},{8,16},{16,24},{24,0},{1,9},{9,17},{17,25},{25,1},{2,10},{10... | collective-permute-start | bytes 466952 | tf_op jit(solution)/shard_map/ppermute | solution.py:786
  26.2 15.9 %collective-permute-start.4 = (bf16[4,56,512]{2,1,0:T(8,128)(2,1)S(1)}, bf16[4,56,512]{2,1,0:T(8,128)(2,1)S(1)}, u32[]{:S(2)}, u32[]{:S(2)}) collective-permute-start(bf16[4,56,512]{2,1,0:T(8,128)(2,1)S(1)} %pad_maximum_fusion.1), channel_id=1, source_target_pairs={{0,4},{1,5},{2,6},{3,7},{4,0},{5,1},{6,2},{7,3},{8,12},{9,13},{10,... | collective-permute-start | bytes 688136 | tf_op jit(solution)/shard_map/ppermute | solution.py:782
  27.8 15.9 %collective-permute-start.3 = (bf16[4,56,512]{2,1,0:T(8,128)(2,1)S(1)}, bf16[4,56,512]{2,1,0:T(8,128)(2,1)S(1)}, u32[]{:S(2)}, u32[]{:S(2)}) collective-permute-start(bf16[4,56,512]{2,1,0:T(8,128)(2,1)S(1)} %pad_maximum_fusion.1), channel_id=1, source_target_pairs={{0,2},{1,3},{2,0},{3,1},{4,6},{5,7},{6,4},{7,5},{8,10},{9,11},{10,... | collective-permute-start | bytes 688136 | tf_op jit(solution)/shard_map/ppermute | solution.py:782
  38.5 35.0 %collective-permute-start.13 = (bf16[4,152,512]{2,1,0:T(8,128)(2,1)S(1)}, bf16[4,152,512]{2,1,0:T(8,128)(2,1)S(1)}, u32[]{:S(2)}, u32[]{:S(2)}) collective-permute-start(bf16[4,152,512]{2,1,0:T(8,128)(2,1)S(1)} %pad_maximum_fusion), channel_id=1, source_target_pairs={{0,6},{1,7},{2,4},{3,5},{4,2},{5,3},{6,0},{7,1},{8,14},{9,15},{10,... | collective-permute-start | bytes 1867784 | tf_op jit(solution)/shard_map/ppermute | solution.py:782
  41.0 31.5 %collective-permute-start.12 = (bf16[4,152,512]{2,1,0:T(8,128)(2,1)S(1)}, bf16[4,152,512]{2,1,0:T(8,128)(2,1)S(1)}, u32[]{:S(2)}, u32[]{:S(2)}) collective-permute-start(bf16[4,152,512]{2,1,0:T(8,128)(2,1)S(1)} %pad_maximum_fusion), channel_id=1, source_target_pairs={{0,4},{1,5},{2,6},{3,7},{4,0},{5,1},{6,2},{7,3},{8,12},{9,13},{10,... | collective-permute-start | bytes 1867784 | tf_op jit(solution)/shard_map/ppermute | solution.py:782
  41.5 30.2 %collective-permute-start.11 = (bf16[4,152,512]{2,1,0:T(8,128)(2,1)S(1)}, bf16[4,152,512]{2,1,0:T(8,128)(2,1)S(1)}, u32[]{:S(2)}, u32[]{:S(2)}) collective-permute-start(bf16[4,152,512]{2,1,0:T(8,128)(2,1)S(1)} %pad_maximum_fusion), channel_id=1, source_target_pairs={{0,2},{1,3},{2,0},{3,1},{4,6},{5,7},{6,4},{7,5},{8,10},{9,11},{10,... | collective-permute-start | bytes 1867784 | tf_op jit(solution)/shard_map/ppermute | solution.py:782
  42.1 27.3 %collective-permute-start.6 = (bf16[2,56,512]{2,1,0:T(8,128)(2,1)S(1)}, bf16[2,56,512]{2,1,0:T(8,128)(2,1)S(1)}, u32[]{:S(2)}, u32[]{:S(2)}) collective-permute-start(bf16[2,56,512]{2,1,0:T(8,128)(2,1)S(1)} %slice.138), channel_id=1, source_target_pairs={{0,2},{1,3},{2,0},{3,1},{4,6},{5,7},{6,4},{7,5},{8,10},{9,11},{10,... | collective-permute-start | bytes 344072 | tf_op jit(solution)/shard_map/ppermute | solution.py:782
  43.7 25.7 %collective-permute-start.5 = (bf16[2,56,512]{2,1,0:T(8,128)(2,1)S(1)}, bf16[2,56,512]{2,1,0:T(8,128)(2,1)S(1)}, u32[]{:S(2)}, u32[]{:S(2)}) collective-permute-start(bf16[2,56,512]{2,1,0:T(8,128)(2,1)S(1)} %slice.137), channel_id=1, source_target_pairs={{0,4},{1,5},{2,6},{3,7},{4,0},{5,1},{6,2},{7,3},{8,12},{9,13},{10,... | collective-permute-start | bytes 344072 | tf_op jit(solution)/shard_map/ppermute | solution.py:782
  69.5 5.3 %copy-start.5 = (bf16[16,56,512]{2,1,0:T(8,128)(2,1)}, bf16[16,56,512]{2,1,0:T(8,128)(2,1)S(1)}, u32[]{:S(2)}) copy-start(bf16[16,56,512]{2,1,0:T(8,128)(2,1)S(1)} %constant_dynamic-update-slice_fusion.near_blocks) | copy-start | bytes 2752516
  69.5 5.3 %collective-permute-start.7 = (bf16[16,56,512]{2,1,0:T(8,128)(2,1)S(1)}, bf16[16,56,512]{2,1,0:T(8,128)(2,1)}, u32[]{:S(2)}, u32[]{:S(2)}) collective-permute-start(bf16[16,56,512]{2,1,0:T(8,128)(2,1)S(1)} %constant_dynamic-update-slice_fusion.near_blocks), channel_id=1, source_target_pairs={{0,1},{1,0},{2,3},{3,2},{4,5},{5,4},{6,7},{7,6},{8,9},{9,8},{10,11... | collective-permute-start | bytes 2752520 | tf_op jit(solution)/shard_map/ppermute | solution.py:782
  74.4 42.9 %collective-permute-start.14 = (bf16[16,152,512]{2,1,0:T(8,128)(2,1)}, bf16[16,152,512]{2,1,0:T(8,128)(2,1)}, u32[]{:S(2)}, u32[]{:S(2)}) collective-permute-start(bf16[16,152,512]{2,1,0:T(8,128)(2,1)} %constant_dynamic-update-slice_fusion.8.near_blocks), channel_id=1, source_target_pairs={{0,1},{1,0},{2,3},{3,2},{4,5},{5,4},{6,7},{7,6},{8,9},{9,8},{10,11... | collective-permute-start | bytes 7471112 | tf_op jit(solution)/shard_map/ppermute | solution.py:782
  264.6 2.7 collective-permute-start.15
  264.8 23.8 %collective-permute-start.21 = (bf16[16,152,512]{2,1,0:T(8,128)(2,1)}, bf16[16,152,512]{2,1,0:T(8,128)(2,1)S(1)}, u32[]{:S(2)}, u32[]{:S(2)}) collective-permute-start(bf16[16,152,512]{2,1,0:T(8,128)(2,1)} %get-tuple-element.43), channel_id=1, source_target_pairs={{0,1},{1,0},{2,3},{3,2},{4,5},{5,4},{6,7},{7,6},{8,9},{9,8},{10,11... | collective-permute-start | bytes 7471112 | tf_op jit(solution)/shard_map/ppermute | solution.py:782
  268.8 19.8 %copy-start = (bf16[16,152,512]{2,1,0:T(8,128)(2,1)S(1)}, bf16[16,152,512]{2,1,0:T(8,128)(2,1)}, u32[]{:S(2)}) copy-start(bf16[16,152,512]{2,1,0:T(8,128)(2,1)} %get-tuple-element.42) | copy-start | bytes 7471108
  268.9 12.6 %collective-permute-start.16 = (bf16[2,4,56,512]{3,2,1,0:T(8,128)(2,1)S(1)}, bf16[2,4,56,512]{3,2,1,0:T(8,128)(2,1)S(1)}, u32[]{:S(2)}, u32[]{:S(2)}) collective-permute-start(bf16[2,4,56,512]{3,2,1,0:T(8,128)(2,1)S(1)} %bitcast.90), channel_id=1, source_target_pairs={{0,4},{1,5},{2,6},{3,7},{4,0},{5,1},{6,2},{7,3},{8,12},{9,13},{10,... | collective-permute-start | bytes 1376264 | tf_op jit(solution)/shard_map/ppermute | solution.py:782
  281.6 6.9 %collective-permute-start.17 = (bf16[4,56,512]{2,1,0:T(8,128)(2,1)S(1)}, bf16[4,56,512]{2,1,0:T(8,128)(2,1)S(1)}, u32[]{:S(2)}, u32[]{:S(2)}) collective-permute-start(bf16[4,56,512]{2,1,0:T(8,128)(2,1)S(1)} %slice_bitcast_fusion), channel_id=1, source_target_pairs={{0,2},{1,3},{2,0},{3,1},{4,6},{5,7},{6,4},{7,5},{8,10},{9,11},{10,... | collective-permute-start | bytes 688136 | tf_op jit(solution)/shard_map/ppermute | solution.py:782
  290.7 17.3 %collective-permute-start.22 = (bf16[4,152,512]{2,1,0:T(8,128)(2,1)}, bf16[4,152,512]{2,1,0:T(8,128)(2,1)}, u32[]{:S(2)}, u32[]{:S(2)}) collective-permute-start(bf16[4,152,512]{2,1,0:T(8,128)(2,1)} %get-tuple-element.44), channel_id=1, source_target_pairs={{0,2},{1,3},{2,0},{3,1},{4,6},{5,7},{6,4},{7,5},{8,10},{9,11},{10,... | collective-permute-start | bytes 1867784 | tf_op jit(solution)/shard_map/ppermute | solution.py:782
  292.2 27.5 %collective-permute-start.24 = (bf16[4,152,512]{2,1,0:T(8,128)(2,1)}, bf16[4,152,512]{2,1,0:T(8,128)(2,1)}, u32[]{:S(2)}, u32[]{:S(2)}) collective-permute-start(bf16[4,152,512]{2,1,0:T(8,128)(2,1)} %get-tuple-element.45), channel_id=1, source_target_pairs={{0,6},{1,7},{2,4},{3,5},{4,2},{5,3},{6,0},{7,1},{8,14},{9,15},{10,... | collective-permute-start | bytes 1867784 | tf_op jit(solution)/shard_map/ppermute | solution.py:782
  293.6 27.2 %collective-permute-start.23 = (bf16[4,152,512]{2,1,0:T(8,128)(2,1)S(1)}, bf16[4,152,512]{2,1,0:T(8,128)(2,1)}, u32[]{:S(2)}, u32[]{:S(2)}) collective-permute-start(bf16[4,152,512]{2,1,0:T(8,128)(2,1)S(1)} %get-tuple-element.46), channel_id=1, source_target_pairs={{0,4},{1,5},{2,6},{3,7},{4,0},{5,1},{6,2},{7,3},{8,12},{9,13},{10,... | collective-permute-start | bytes 1867784 | tf_op jit(solution)/shard_map/ppermute | solution.py:782
  294.8 6.1 %collective-permute-start.18 = (bf16[56,512]{1,0:T(8,128)(2,1)S(1)}, bf16[56,512]{1,0:T(8,128)(2,1)S(1)}, u32[]{:S(2)}, u32[]{:S(2)}) collective-permute-start(bf16[56,512]{1,0:T(8,128)(2,1)S(1)} %get-tuple-element.57), channel_id=1, source_target_pairs={{0,8},{8,16},{16,24},{24,0},{1,9},{9,17},{17,25},{25,1},{2,10},{10... | collective-permute-start | bytes 172040 | tf_op jit(solution)/shard_map/ppermute | solution.py:786
  295.7 6.3 %collective-permute-start.20 = (bf16[56,512]{1,0:T(8,128)(2,1)}, bf16[56,512]{1,0:T(8,128)(2,1)S(1)}, u32[]{:S(2)}, u32[]{:S(2)}) collective-permute-start(bf16[56,512]{1,0:T(8,128)(2,1)} %get-tuple-element.58), channel_id=1, source_target_pairs={{0,24},{8,0},{16,8},{24,16},{1,25},{9,1},{17,9},{25,17},{2,26},{10... | collective-permute-start | bytes 172040 | tf_op jit(solution)/shard_map/ppermute | solution.py:786
  300.9 5.2 %collective-permute-start.19 = (bf16[56,512]{1,0:T(8,128)(2,1)S(1)}, bf16[56,512]{1,0:T(8,128)(2,1)}, u32[]{:S(2)}, u32[]{:S(2)}) collective-permute-start(bf16[56,512]{1,0:T(8,128)(2,1)S(1)} %get-tuple-element.59), channel_id=1, source_target_pairs={{0,16},{8,24},{16,0},{24,8},{1,17},{9,25},{17,1},{25,9},{2,18},{10... | collective-permute-start | bytes 172040 | tf_op jit(solution)/shard_map/ppermute | solution.py:786
  322.6 7.6 %collective-permute-start.25 = (bf16[152,512]{1,0:T(8,128)(2,1)S(1)}, bf16[152,512]{1,0:T(8,128)(2,1)S(1)}, u32[]{:S(2)}, u32[]{:S(2)}) collective-permute-start(bf16[152,512]{1,0:T(8,128)(2,1)S(1)} %get-tuple-element.49), channel_id=1, source_target_pairs={{0,8},{8,16},{16,24},{24,0},{1,9},{9,17},{17,25},{25,1},{2,10},{10... | collective-permute-start | bytes 466952 | tf_op jit(solution)/shard_map/ppermute | solution.py:786
  323.5 8.0 %collective-permute-start.27 = (bf16[152,512]{1,0:T(8,128)(2,1)S(1)}, bf16[152,512]{1,0:T(8,128)(2,1)S(1)}, u32[]{:S(2)}, u32[]{:S(2)}) collective-permute-start(bf16[152,512]{1,0:T(8,128)(2,1)S(1)} %get-tuple-element.50), channel_id=1, source_target_pairs={{0,24},{8,0},{16,8},{24,16},{1,25},{9,1},{17,9},{25,17},{2,26},{10... | collective-permute-start | bytes 466952 | tf_op jit(solution)/shard_map/ppermute | solution.py:786
  326.5 10.2 %collective-permute-start.26 = (bf16[152,512]{1,0:T(8,128)(2,1)S(1)}, bf16[152,512]{1,0:T(8,128)(2,1)S(1)}, u32[]{:S(2)}, u32[]{:S(2)}) collective-permute-start(bf16[152,512]{1,0:T(8,128)(2,1)S(1)} %get-tuple-element.51), channel_id=1, source_target_pairs={{0,16},{8,24},{16,0},{24,8},{1,17},{9,25},{17,1},{25,9},{2,18},{10... | collective-permute-start | bytes 466952 | tf_op jit(solution)/shard_map/ppermute | solution.py:786
